TPU v7x, 32 devices: a whole 2x2x4 slice. The times are simulated.
32 devices in a mesh: dp: 16 (over z, y, core), hst: 2 (over x).
Axes of the slice: x: 2, y: 2, z: 4, core: 2. Of those that a mesh axis runs over, the one named last changes fastest.
Arguments:
- image_embeds: float32 [16, 2, 256, 1024], P('dp', 'hst'), may hold values from -16 to 16
- text_embeds: float32 [16, 2, 256, 1024], P('dp', 'hst'), may hold values from -16 to 16
Outputs:
- mean_loss: float32 [], replicated
- image_grads: float32 [16, 2, 256, 1024], P('dp', 'hst')
- text_grads: float32 [16, 2, 256, 1024], P('dp', 'hst')
All inputs are finite; a program needn't handle non-finite values.
Results may differ from a plain program's by a relative error of at most 0.000068.
Values sent between devices are 32-bit elements; how exact they have to be, the bound alone decides.
No kernel may reach another device: no remote copies, remote signals or barrier semaphores. Data moves between devices by JAX's collectives and lax.ppermute only.
A program may use at most 64 MiB of HBM per device.

v0:
```python
import jax
import jax.numpy as jnp
from jax import lax
from jax.sharding import PartitionSpec as P

logit_scale = 0.03125
highest = lax.Precision.HIGHEST


def from_behind(value, axis, steps):
    count = lax.axis_size(axis)
    pairs = [(source, (source + steps) % count) for source in range(count)]
    return lax.ppermute(value, axis, pairs)


def block_logits(left_side, right_side):
    return logit_scale * lax.dot_general(
        left_side,
        right_side,
        (((1,), (1,)), ((), ())),
        precision=highest,
        preferred_element_type=jnp.float32,
    )


def left_product(coefficients, right_side):
    return jnp.dot(coefficients, right_side, precision=highest, preferred_element_type=jnp.float32)


def right_product(coefficients, left_side):
    return lax.dot_general(
        coefficients,
        left_side,
        (((0,), (0,)), ((), ())),
        precision=highest,
        preferred_element_type=jnp.float32,
    )


def joint_logsum(former, latter, reduced):
    largest = jnp.maximum(jnp.max(former, axis=reduced), jnp.max(latter, axis=reduced))
    lifted = jnp.expand_dims(largest, reduced)
    return largest + jnp.log(
        jnp.sum(jnp.exp(former - lifted), axis=reduced)
        + jnp.sum(jnp.exp(latter - lifted), axis=reduced)
    )


def single_column_logsum(logits):
    largest = jnp.max(logits, axis=0)
    return largest + jnp.log(jnp.sum(jnp.exp(logits - largest[None, :]), axis=0))


def paired_logsum(former, latter):
    largest = jnp.maximum(former, latter)
    return largest + jnp.log(jnp.exp(former - largest) + jnp.exp(latter - largest))


def weights(logits, row_logsum, column_logsum):
    return 0.5 * (jnp.exp(logits - row_logsum[:, None]) + jnp.exp(logits - column_logsum[None, :]))


def on_device(image_embeds, text_embeds):
    own_images = image_embeds[0, 0]
    own_texts = text_embeds[0, 0]
    row_count = own_images.shape[0]
    earlier_texts = from_behind(own_texts, "dp", 1)
    self_logits = block_logits(own_images, own_texts)
    earlier_logits = block_logits(own_images, earlier_texts)
    row_logsum = joint_logsum(self_logits, earlier_logits, 1)
    identity = (
        lax.broadcasted_iota(jnp.int32, (row_count, row_count), 0)
        == lax.broadcasted_iota(jnp.int32, (row_count, row_count), 1)
    ).astype(jnp.float32)
    self_columns = single_column_logsum(self_logits)
    earlier_columns = single_column_logsum(earlier_logits)
    after_columns = from_behind(earlier_columns, "dp", -1)
    column_logsum = paired_logsum(self_columns, after_columns)
    before_logsum = from_behind(column_logsum, "dp", 1)
    self_weights = weights(self_logits, row_logsum, column_logsum) - identity
    earlier_weights = weights(earlier_logits, row_logsum, before_logsum)
    outgoing = right_product(earlier_weights, own_images)
    incoming = from_behind(outgoing, "dp", -1)
    text_sum = right_product(self_weights, own_images) + incoming
    image_sum = left_product(self_weights, own_texts) + left_product(earlier_weights, earlier_texts)
    positive = jnp.sum(jnp.diagonal(self_logits))
    partial_total = 0.5 * (jnp.sum(row_logsum) + jnp.sum(column_logsum)) - positive
    loss_total = lax.psum(partial_total, ("dp", "hst"))
    batch_rows = row_count * lax.axis_size("dp") * lax.axis_size("hst")
    mean_loss = loss_total / batch_rows
    return (mean_loss, (logit_scale * image_sum)[None, None], (logit_scale * text_sum)[None, None])


def solution(mesh):
    return jax.shard_map(
        on_device,
        mesh=mesh,
        in_specs=(P("dp", "hst", None, None), P("dp", "hst", None, None)),
        out_specs=(P(), P("dp", "hst", None, None), P("dp", "hst", None, None)),
        check_vma=False,
    )
```

profile of v0, /device:TPU:0, one launch (start us, length us, event | category | flops | bytes accessed | tf_op | source)
XLA Modules:
  0.0 86.1 jit_solution(12007273766255028963)
XLA Ops:
  0.6 0.0 copy-start
  0.6 0.5 collective-permute-start
  1.1 0.7 copy-done
  1.9 2.3 %fusion.29 = (f32[256]{0:T(256)S(1)}, f32[256]{0:T(256)S(1)}, f32[256,256]{1,0:T(8,128)S(1)}) fusion(f32[1,1,256,1024]{3,2,1,0:T(8,128)} %param.3, f32[1,1,256,1024]{3,2,1,0:T(8,128)S(1)} %copy-done), kind=kOutput, calls=%fused_computation.46 | convolution fusion | flops 805502464 | bytes 2361344 | tf_op jit(solution)/shard_map/dot_general | solution.py:17
  4.2 14.6 %collective-permute-done = f32[256,1024]{1,0:T(8,128)S(1)} collective-permute-done((f32[256,1024]{1,0:T(8,128)}, f32[256,1024]{1,0:T(8,128)S(1)}, u32[]{:S(2)}, u32[]{:S(2)}) %collective-permute-start) | collective-permute-done | bytes 1048608 | tf_op jit(solution)/shard_map/ppermute | solution.py:13
  18.8 1.1 %fusion.30 = (f32[256]{0:T(256)S(1)}, f32[256]{0:T(256)S(1)}, f32[256,256]{1,0:T(8,128)S(1)}) fusion(f32[256,1024]{1,0:T(8,128)S(1)} %collective-permute-done, f32[1,1,256,1024]{3,2,1,0:T(8,128)S(1)} %copy-done), kind=kOutput, calls=%fused_computation.47 | convolution fusion | flops 805502464 | bytes 2361344 | tf_op jit(solution)/shard_map/dot_general | solution.py:17
  20.0 0.3 exponential_reduce_fusion
  20.3 0.1 collective-permute-start.1
  20.3 1.3 %collective-permute-done.1 = f32[256]{0:T(256)S(1)} collective-permute-done((f32[256]{0:T(256)S(1)}, f32[256]{0:T(256)S(1)}, u32[]{:S(2)}, u32[]{:S(2)}) %collective-permute-start.1) | collective-permute-done | bytes 1056 | tf_op jit(solution)/shard_map/ppermute | solution.py:13
  21.6 0.7 fusion.31
  22.3 0.0 collective-permute-start.2
  22.3 0.6 fusion.32
  22.9 5.1 %collective-permute-done.2 = f32[256]{0:T(256)S(1)} collective-permute-done((f32[256]{0:T(256)S(1)}, f32[256]{0:T(256)S(1)}, u32[]{:S(2)}, u32[]{:S(2)}) %collective-permute-start.2) | collective-permute-done | bytes 1056 | tf_op jit(solution)/shard_map/ppermute | solution.py:13
  28.0 0.0 copy-done.2
  28.0 2.1 %fusion.4 = f32[256,1024]{1,0:T(8,128)} fusion(f32[1,1,256,1024]{3,2,1,0:T(8,128)S(1)} %copy-done, f32[256,256]{1,0:T(8,128)S(1)} %get-tuple-element.18, f32[256]{0:T(256)S(1)} %collective-permute-done.2, f32[256]{0:T(256)S(1)} %get-tuple-element.14), kind=kOutput, calls=%fused_computation.9 | convolution fusion | flops 805568512 | bytes 2361344 | tf_op jit(solution)/shard_map/dot_general | solution.py:31
  30.1 0.0 collective-permute-start.3
  30.1 2.3 %gather_fusion = f32[256]{0:T(256)S(1)} fusion(f32[256,256]{1,0:T(8,128)S(1)} %get-tuple-element.17, s32[256]{0:T(256)S(1)} %bitcast.27), kind=kCustom, calls=%fused_computation | custom fusion | bytes 4096 | tf_op jit(solution)/shard_map/jit(diagonal)/cond/branch_0_fun/gather | solution.py:86
  32.5 0.6 reduce_sum.69
  35.0 42.8 %psum.7 = f32[]{:T(128)} all-reduce(f32[]{:T(128)S(6)} %sub.81), channel_id=1, replica_groups=mesh['dp'=16,'hst'=2] {'dp','hst'}, use_global_device_ids=true, to_apply=%region_11.12 | all-reduce | flops 1 | bytes 8 | tf_op jit(solution)/shard_map/psum | solution.py:88
  78.5 0.0 copy-start.3
  78.5 1.1 %fusion.9 = f32[256,1024]{1,0:T(8,128)S(1)} fusion(f32[256,256]{1,0:T(8,128)S(1)} %get-tuple-element.17, f32[256]{0:T(256)S(1)} %get-tuple-element.12, f32[256]{0:T(256)S(1)} %get-tuple-element.14, f32[1,1,256,1024]{3,2,1,0:T(8,128)S(1)} %copy-done.1), kind=kOutput, calls=%fused_computation.21 | convolution fusion | flops 805765120 | bytes 2361344 | tf_op jit(solution)/shard_map/dot_general | solution.py:27
  79.6 2.1 %fusion.3 = f32[1,1,256,1024]{3,2,1,0:T(8,128)} fusion(f32[256,1024]{1,0:T(8,128)S(1)} %fusion.9, f32[256,1024]{1,0:T(8,128)S(1)} %collective-permute-done, f32[256,256]{1,0:T(8,128)S(1)} %copy-done.3, f32[256]{0:T(256)S(1)} %collective-permute-done.2, f32[256]{0:T(256)S(1)} %get-tuple-element.14), kind=kOutput, calls=%fused_computation.6 | convolution fusion | flops 806092800 | bytes 3409920 | tf_op jit(solution)/shard_map/dot_general | solution.py:27
  81.7 0.0 collective-permute-done.3
  81.7 3.3 %fusion.1 = f32[1,1,256,1024]{3,2,1,0:T(8,128)} fusion(f32[256,1024]{1,0:T(8,128)} %collective-permute-done.3, f32[1,1,256,1024]{3,2,1,0:T(8,128)S(1)} %copy-done, f32[256,256]{1,0:T(8,128)S(1)} %get-tuple-element.17, f32[256]{0:T(256)S(1)} %get-tuple-element.12, f32[256]{0:T(256)S(1)} %get-tuple-element.14), kind=kOutput, calls=%fused_computation.3 | convolution fusion | flops 806289408 | bytes 3409920 | tf_op jit(solution)/shard_map/dot_general | solution.py:31
  (7 shorter events, 0.0 us)
Async XLA Ops:
  0.6 1.2 %copy-start = (f32[1,1,256,1024]{3,2,1,0:T(8,128)S(1)}, f32[1,1,256,1024]{3,2,1,0:T(8,128)}, u32[]{:S(2)}) copy-start(f32[1,1,256,1024]{3,2,1,0:T(8,128)} %param.2) | copy-start | bytes 3145732
  0.6 18.2 %collective-permute-start = (f32[256,1024]{1,0:T(8,128)}, f32[256,1024]{1,0:T(8,128)S(1)}, u32[]{:S(2)}, u32[]{:S(2)}) collective-permute-start(f32[256,1024]{1,0:T(8,128)} %bitcast.28), channel_id=1, source_target_pairs={{0,2},{2,4},{4,6},{6,8},{8,10},{10,12},{12,14},{14,16},{16,18},{18... | collective-permute-start | bytes 3145736 | tf_op jit(solution)/shard_map/ppermute | solution.py:13
  20.0 8.0 %copy-start.2 = (f32[256,256]{1,0:T(8,128)}, f32[256,256]{1,0:T(8,128)S(1)}, u32[]{:S(2)}) copy-start(f32[256,256]{1,0:T(8,128)S(1)} %get-tuple-element.18) | copy-start | bytes 786436
  20.3 1.4 %collective-permute-start.1 = (f32[256]{0:T(256)S(1)}, f32[256]{0:T(256)S(1)}, u32[]{:S(2)}, u32[]{:S(2)}) collective-permute-start(f32[256]{0:T(256)S(1)} %log_add_fusion.1), channel_id=1, source_target_pairs={{0,30},{2,0},{4,2},{6,4},{8,6},{10,8},{12,10},{14,12},{16,14},{18,... | collective-permute-start | bytes 3080 | tf_op jit(solution)/shard_map/ppermute | solution.py:13
  22.3 5.7 %collective-permute-start.2 = (f32[256]{0:T(256)S(1)}, f32[256]{0:T(256)S(1)}, u32[]{:S(2)}, u32[]{:S(2)}) collective-permute-start(f32[256]{0:T(256)S(1)} %get-tuple-element.12), channel_id=1, source_target_pairs={{0,2},{2,4},{4,6},{6,8},{8,10},{10,12},{12,14},{14,16},{16,18},{18... | collective-permute-start | bytes 3080 | tf_op jit(solution)/shard_map/ppermute | solution.py:13
  30.1 48.3 %copy-start.1 = (f32[1,1,256,1024]{3,2,1,0:T(8,128)S(1)}, f32[1,1,256,1024]{3,2,1,0:T(8,128)}, u32[]{:S(2)}) copy-start(f32[1,1,256,1024]{3,2,1,0:T(8,128)} %param.3) | copy-start | bytes 3145732
  30.1 51.5 %collective-permute-start.3 = (f32[256,1024]{1,0:T(8,128)}, f32[256,1024]{1,0:T(8,128)}, u32[]{:S(2)}, u32[]{:S(2)}) collective-permute-start(f32[256,1024]{1,0:T(8,128)} %fusion.4), channel_id=1, source_target_pairs={{0,30},{2,0},{4,2},{6,4},{8,6},{10,8},{12,10},{14,12},{16,14},{18,... | collective-permute-start | bytes 3145736 | tf_op jit(solution)/shard_map/ppermute | solution.py:13
  78.5 1.1 %copy-start.3 = (f32[256,256]{1,0:T(8,128)S(1)}, f32[256,256]{1,0:T(8,128)}, u32[]{:S(2)}) copy-start(f32[256,256]{1,0:T(8,128)} %copy-done.2) | copy-start | bytes 786436
where the time goes:
time: 86.5 us; the launch traced here: 86.1 us
  blocking collectives  42.8 us (49%)
  waiting for transfers between devices  21 us (24%)
  matrix products  12.1 us (14%)
  between operations  4.4 us (5%)
  local copies, waits for them, and re-layouts  3.07 us (4%)
  other arithmetic  2.19 us (3%)
    psum x1, blocking collectives, on_device(): loss_total = lax.psum(partial_total, ('dp', 'hst'))  42.8 us
    ppermute x4, waiting for transfers between devices, from_behind(): return lax.ppermute(value, axis, pairs)  21 us
    dot_general x2, matrix products, right_product(): lax.dot_general(coefficients, left_side, (((0,), (0,)), ((), ())), precis...  5.46 us
    dot_general x2, matrix products, block_logits(): lax.dot_general(left_side, right_side, (((1,), (1,)), ((), ())), precisio...  3.46 us
    dot_general x2, matrix products, left_product(): jnp.dot(coefficients, right_side, precision=highest, preferred_element_ty...  3.17 us
    gather x1, local copies, waits for them, and re-layouts, on_device(): positive = jnp.sum(jnp.diagonal(self_logits))  2.34 us
  transfers between devices with their start and end apart: 4, of which 3 were waited for; matrix products, arithmetic and copies ran while one was open for 11% of the time, Pallas kernels for 0%

commit v1 on v0

v1 whole, which is shorter than its diff:
```python
import jax
import jax.numpy as jnp
from jax import lax
from jax.experimental import pallas as pl
from jax.experimental.pallas import tpu as pltpu
from jax.sharding import PartitionSpec as P

logit_scale = 0.03125
f32, bf16 = jnp.float32, jnp.bfloat16
LANES = 128


def from_behind(value, axis, steps):
    count = lax.axis_size(axis)
    pairs = [(source, (source + steps) % count) for source in range(count)]
    return lax.ppermute(value, axis, pairs)


def split(value):
    high = value.astype(bf16)
    rest = value - high.astype(f32)
    middle = rest.astype(bf16)
    low = (rest - middle.astype(f32)).astype(bf16)
    return high, middle, low


PAIRS = ((2, 0), (1, 1), (0, 2), (1, 0), (0, 1), (0, 0))


def rows_by_rows(left, right):
    return lax.dot_general(
        jnp.concatenate([left[one] for one, _ in PAIRS], axis=1),
        jnp.concatenate([right[other] for _, other in PAIRS], axis=1),
        (((1,), (1,)), ((), ())),
        preferred_element_type=f32,
    )


def left_parts(left):
    parts = split(left)
    return jnp.concatenate([parts[one] for one, _ in PAIRS], axis=1)


def rows_by_columns(left, right):
    return jnp.dot(left, jnp.concatenate([right[other] for _, other in PAIRS], axis=0), preferred_element_type=f32)


def store_parts(stacked, value):
    for place, part in enumerate(split(value)):
        stacked[place] = part


def logsum(logits, axis):
    largest = jnp.max(logits, axis=axis, keepdims=True)
    return largest + jnp.log(jnp.sum(jnp.exp(logits - largest), axis=axis, keepdims=True))


def paired_logsum(former, latter):
    largest = jnp.maximum(former, latter)
    return largest + jnp.log(jnp.exp(former - largest) + jnp.exp(latter - largest))


def diagonal_mask(count):
    shape = (count, count)
    return lax.broadcasted_iota(jnp.int32, shape, 0) == lax.broadcasted_iota(jnp.int32, shape, 1)


def as_row(column, diagonal):
    return jnp.sum(jnp.where(diagonal, column, 0.0), axis=0, keepdims=True)


def as_column(row, diagonal):
    return jnp.sum(jnp.where(diagonal, row, 0.0), axis=1, keepdims=True)


def total(values):
    return jnp.sum(jnp.sum(values, axis=1, keepdims=True), axis=0, keepdims=True)


def unpack(message, place, count):
    rows = count // LANES
    return jnp.concatenate([message[place * rows + k : place * rows + k + 1, :] for k in range(rows)], axis=1)


def start(pairs, semaphores):
    copies = [pltpu.make_async_copy(source, target, semaphores.at[k]) for k, (source, target) in enumerate(pairs)]
    for copy in copies:
        copy.start()
    return copies


def self_kernel(
    images, texts,
    logits, image_parts, text_parts, row_part, positive, column_part, text_store,
    image_in, text_in, semaphores,
):
    copies = start([(images, image_in), (texts, text_in)], semaphores)
    copies[0].wait()
    store_parts(image_parts, image_in[...])
    copies[1].wait()
    store_parts(text_parts, text_in[...])
    copies = start([(text_parts, text_store)], semaphores.at[2:3])
    block = logit_scale * rows_by_rows(image_parts, text_parts)
    diagonal = diagonal_mask(block.shape[0])
    logits[...] = block
    row_part[...] = as_row(logsum(block, 1), diagonal)
    column_part[...] = logsum(block, 0)
    positive[...] = total(jnp.where(diagonal, block, 0.0))
    copies[0].wait()


def earlier_kernel(
    image_parts, text_parts, earlier_texts, logits, self_rows, self_columns, before_columns, positive,
    messages, image_part, row_term, column_term,
    earlier_parts, image_out, row_out, column_out, semaphores,
):
    store_parts(earlier_parts, earlier_texts[...])
    block = logit_scale * rows_by_rows(image_parts, earlier_parts)
    count, width = image_out.shape
    diagonal = diagonal_mask(count)
    own = logits[...]
    rows = paired_logsum(as_column(self_rows[...], diagonal), logsum(block, 1))
    columns = paired_logsum(before_columns[...], logsum(block, 0))
    messages[...] = jnp.broadcast_to(0.5 * (total(rows) + total(columns)) - positive[...], messages.shape)
    by_rows = 0.5 * jnp.exp(own - rows) - jnp.where(diagonal, 1.0, 0.0)
    by_columns = 0.5 * jnp.exp(own - self_columns[...])
    earlier_left = left_parts(0.5 * (jnp.exp(block - rows) + jnp.exp(block - columns)))
    row_left, row_down, column_down = left_parts(by_rows), left_parts(by_rows.T), left_parts(by_columns.T)
    half = width // 2
    outs = []
    for k in range(2):
        part = slice(k * half, (k + 1) * half)
        row_out[:, part] = rows_by_columns(row_down, image_parts.at[:, :, part])
        column_out[:, part] = rows_by_columns(column_down, image_parts.at[:, :, part])
        image_out[:, part] = rows_by_columns(earlier_left, earlier_parts.at[:, :, part]) + rows_by_columns(
            row_left, text_parts.at[:, :, part]
        )
        outs += start(
            [
                (source.at[:, part], target.at[:, part])
                for source, target in ((row_out, row_term), (column_out, column_term), (image_out, image_part))
            ],
            semaphores.at[3 * k : 3 * k + 3],
        )
    for copy in outs:
        copy.wait()


def image_kernel(
    text_store, later_images, logits, later_rows, self_columns, image_part,
    left, later_parts, columns_out, image_grads,
    text_parts, part_in, image_out, semaphores,
):
    copies = start([(text_store, text_parts), (image_part, part_in)], semaphores)
    count, width = image_out.shape
    diagonal = diagonal_mask(count)
    store_parts(later_parts, later_images[...])
    copies[0].wait()
    block = logit_scale * rows_by_rows(text_parts, later_parts)
    rows = paired_logsum(later_rows[...], logsum(block, 0))
    columns = paired_logsum(as_column(self_columns[...], diagonal), logsum(block, 1))
    left[...] = left_parts(0.5 * (jnp.exp(block - rows) + jnp.exp(block - columns)))
    across = as_row(columns, diagonal)
    columns_out[...] = across
    own_left = left_parts(0.5 * jnp.exp(logits[...] - across))
    copies[1].wait()
    outs = []
    half = width // 2
    for k in range(2):
        part = slice(k * half, (k + 1) * half)
        image_out[:, part] = logit_scale * (part_in[:, part] + rows_by_columns(own_left, text_parts.at[:, :, part]))
        outs += start([(image_out.at[:, part], image_grads.at[:, part])], semaphores.at[2 + k : 3 + k])
    for copy in outs:
        copy.wait()


def text_kernel(
    left, later_parts, columns, self_columns, row_term, column_term, messages,
    mean_loss, text_grads,
    row_in, column_in, text_out, semaphores,
):
    copies = start([(row_term, row_in), (column_term, column_in)], semaphores)
    count, width = text_out.shape
    mean_loss[...] = total(messages[:, 0, 0:1]) / (count * messages.shape[0])
    scale = as_column(jnp.exp(self_columns[...] - columns[...]), diagonal_mask(count))
    for copy in copies:
        copy.wait()
    outs = []
    half = width // 2
    for k in range(2):
        part = slice(k * half, (k + 1) * half)
        terms = rows_by_columns(left[...], later_parts.at[:, :, part])
        text_out[:, part] = logit_scale * (row_in[:, part] + scale * column_in[:, part] + terms)
        outs += start([(text_out.at[:, part], text_grads.at[:, part])], semaphores.at[2 + k : 3 + k])
    for copy in outs:
        copy.wait()


VM, HB, SM = pl.BlockSpec(memory_space=pltpu.VMEM), pl.BlockSpec(memory_space=pltpu.HBM), pl.BlockSpec(memory_space=pltpu.SMEM)


def call(kernel, products, ins, outs, scratch, copies):
    def shape_of(place, shape, dtype):
        if place is HB:
            return pltpu.HBM(shape, dtype)
        return jax.ShapeDtypeStruct(shape, dtype)

    run = pl.pallas_call(
        kernel,
        out_shape=[shape_of(*out) for out in outs],
        in_specs=ins,
        out_specs=[out[0] for out in outs],
        scratch_shapes=[pltpu.VMEM(shape, dtype) for shape, dtype in scratch]
        + ([pltpu.SemaphoreType.DMA((copies,))] if copies else []),
        compiler_params=pltpu.CompilerParams(vmem_limit_bytes=24 << 20),
        cost_estimate=pl.CostEstimate(
            flops=products * 12 * 256 * 256 * 1024, bytes_accessed=4 << 20, transcendentals=1 << 18
        ),
    )

    def pinned(*values):
        return run(
            *[pltpu.with_memory_space_constraint(v, pltpu.HBM) if spec is HB else v for v, spec in zip(values, ins)]
        )

    return pinned


def on_device(image_embeds, text_embeds):
    images, texts = image_embeds[0, 0], text_embeds[0, 0]
    count, width = images.shape
    square, row, whole = (count, count), (1, count), (count, width)
    parts, left = ((3, count, width), bf16), ((count, len(PAIRS) * count), bf16)
    devices = lax.axis_size("dp") * lax.axis_size("hst")
    earlier_texts = from_behind(texts, "dp", 1)
    logits, image_parts, text_parts, self_rows, positive, self_columns, text_store = call(
        self_kernel,
        1,
        [HB, HB],
        [(VM, square, f32), (VM, *parts), (VM, *parts), (VM, row, f32), (VM, (1, 1), f32), (VM, row, f32), (HB, *parts)],
        [(whole, f32), (whole, f32)],
        3,
    )(images, texts)
    before_columns = from_behind(self_columns, "dp", 1)
    later_rows = from_behind(self_rows, "dp", -1)
    earlier_texts, images, before_columns, later_rows = lax.optimization_barrier(
        (earlier_texts, images, before_columns, later_rows)
    )
    later_images = from_behind(images, "dp", -1)
    messages, image_part, row_term, column_term = call(
        earlier_kernel,
        5,
        [VM] * 8,
        [(VM, (devices, 1, LANES), f32)] + [(HB, whole, f32)] * 3,
        [parts] + [(whole, f32)] * 3,
        6,
    )(image_parts, text_parts, earlier_texts, logits, self_rows, self_columns, before_columns, positive)
    messages = lax.all_to_all(messages, ("dp", "hst"), 0, 0, tiled=True)
    left, later_parts, columns, image_grads = call(
        image_kernel,
        2,
        [HB, VM, VM, VM, VM, HB],
        [(VM, *left), (VM, *parts), (VM, row, f32), (HB, whole, f32)],
        [parts, (whole, f32), (whole, f32)],
        4,
    )(text_store, later_images, logits, later_rows, self_columns, image_part)
    mean_loss, text_grads = call(
        text_kernel,
        1,
        [VM] * 4 + [HB, HB, VM],
        [(VM, (1, 1), f32), (HB, whole, f32)],
        [(whole, f32)] * 3,
        4,
    )(left, later_parts, columns, self_columns, row_term, column_term, messages)
    return mean_loss[0, 0], image_grads[None, None], text_grads[None, None]


def solution(mesh):
    return jax.shard_map(
        on_device,
        mesh=mesh,
        in_specs=(P("dp", "hst", None, None), P("dp", "hst", None, None)),
        out_specs=(P(), P("dp", "hst", None, None), P("dp", "hst", None, None)),
        check_vma=False,
    )
```

time: 86.5 us -> 42.6 us (0.49)
  blocking collectives: 42.8 us -> 0 us
  Pallas kernels: 0 us -> 22.7 us
  waiting for transfers between devices: 21 us -> 8.66 us
  matrix products: 12.1 us -> 0 us
  starting transfers between devices: 0.59 us -> 9.36 us
  between operations: 4.4 us -> 0.71 us
  other arithmetic: 2.19 us -> 0 us
  local copies, waits for them, and re-layouts: 3.07 us -> 0.96 us
    psum x1 -> x0, blocking collectives: 42.8 us -> none  [on_device(): loss_total = lax.psum(partial_total, ('dp', 'hst'))]
    pallas_call x0 -> x4, Pallas kernels: none -> 22.7 us  [pinned(): run(*[pltpu.with_memory_space_constraint(v, pltpu.HBM) if spec is HB else...]
    ppermute x4, waiting for transfers between devices: 21 us -> 8.66 us  [from_behind(): return lax.ppermute(value, axis, pairs)]
    dot_general x6 -> x0, matrix products: 12.1 us -> none  [the longest x2 5.46 us: right_product(): lax.dot_general(coefficients, left_side, (((0,), (0,)), ((), ())), precis...]
    ppermute x4, starting transfers between devices: 0.59 us -> 5.65 us  [from_behind(): return lax.ppermute(value, axis, pairs)]
    all_to_all x0 -> x1, starting transfers between devices: none -> 3.7 us  [on_device(): messages = lax.all_to_all(messages, ('dp', 'hst'), 0, 0, tiled=True)]
    gather x1 -> x0, local copies, waits for them, and re-layouts: 2.34 us -> none  [on_device(): positive = jnp.sum(jnp.diagonal(self_logits))]
    reduce_sum x4 -> x0, other arithmetic: 2.17 us -> none  [the longest x1 0.7 us: on_device(): jnp.sum(column_logsum)]
  transfers between devices with their start and end apart: 4 -> 5, of which waited for: 3 -> 3; matrix products, arithmetic and copies ran while one was open for 11% -> 0% of each run, Pallas kernels for 0% -> 44%
where the time goes in v1:
time: 42.6 us; the launch traced here: 42.3 us
  Pallas kernels  22.7 us (53%)
  starting transfers between devices  9.36 us (22%)
  waiting for transfers between devices  8.66 us (20%)
  local copies, waits for them, and re-layouts  0.96 us (2%)
  between operations  0.71 us (2%)
    pallas_call x4, Pallas kernels, pinned(): run(*[pltpu.with_memory_space_constraint(v, pltpu.HBM) if spec is HB else...  22.7 us
    ppermute x4, waiting for transfers between devices, from_behind(): return lax.ppermute(value, axis, pairs)  8.66 us
    ppermute x4, starting transfers between devices, from_behind(): return lax.ppermute(value, axis, pairs)  5.65 us
    all_to_all x1, starting transfers between devices, on_device(): messages = lax.all_to_all(messages, ('dp', 'hst'), 0, 0, tiled=True)  3.7 us
    unnamed x6, local copies, waits for them, and re-layouts  0.96 us
  transfers between devices with their start and end apart: 5, of which 3 were waited for; matrix products, arithmetic and copies ran while one was open for 0% of the time, Pallas kernels for 44%

profile of v1, /device:TPU:0, one launch (start us, length us, event | category | flops | bytes accessed | tf_op | source)
XLA Modules:
  0.0 42.3 jit_solution(9542303084971650353)
XLA Ops:
  0.6 0.0 copy-start.2
  0.6 0.5 %collective-permute-start = (f32[256,1024]{1,0:T(8,128)}, f32[256,1024]{1,0:T(8,128)S(1)}, u32[]{:S(2)}, u32[]{:S(2)}) collective-permute-start(f32[256,1024]{1,0:T(8,128)} %bitcast.5), channel_id=1, source_target_pairs={{0,2},{2,4},{4,6},{6,8},{8,10},{10,12},{12,14},{14,16},{16,18},{18... | collective-permute-start | bytes 3145736 | tf_op jit(solution)/shard_map/ppermute | solution.py:16
  1.1 4.0 %shard_map.49 = (f32[256,256]{1,0:T(8,128)S(1)}, bf16[3,256,1024]{2,1,0:T(8,128)(2,1)S(1)}, bf16[3,256,1024]{2,1,0:T(8,128)(2,1)S(1)}, f32[1,256]{1,0:T(1,128)S(...) custom-call(f32[256,1024]{1,0:T(8,128)} %bitcast.7, f32[256,1024]{1,0:T(8,128)} %bitcast.6), custom_call_target="tpu_custom_call" | custom-call | flops 805306368 | bytes 4194304 | tf_op jit(solution)/shard_map/pallas_call | solution.py:222
  5.2 0.0 copy-start
  5.2 5.1 %collective-permute-start.2 = (f32[1,256]{1,0:T(1,128)S(1)}, f32[1,256]{1,0:T(1,128)S(1)}, u32[]{:S(2)}, u32[]{:S(2)}) collective-permute-start(f32[1,256]{1,0:T(1,128)S(1)} %get-tuple-element.26.self_rows), channel_id=1, source_target_pairs={{0,30},{2,0},{4,2},{6,4},{8,6},{10,8},{12,10},{14,12},{16,14},{18,... | collective-permute-start | bytes 3080 | tf_op jit(solution)/shard_map/ppermute | solution.py:16
  10.3 0.0 collective-permute-start.1
  10.3 1.3 %collective-permute-done.2.later_rows = f32[1,256]{1,0:T(1,128)S(1)} collective-permute-done((f32[1,256]{1,0:T(1,128)S(1)}, f32[1,256]{1,0:T(1,128)S(1)}, u32[]{:S(2)}, u32[]{:S(2)}) %collective-permute-start.2) | collective-permute-done | bytes 1056 | tf_op jit(solution)/shard_map/ppermute | solution.py:16
  11.6 7.3 %collective-permute-done.1.before_columns = f32[1,256]{1,0:T(1,128)S(1)} collective-permute-done((f32[1,256]{1,0:T(1,128)S(1)}, f32[1,256]{1,0:T(1,128)S(1)}, u32[]{:S(2)}, u32[]{:S(2)}) %collective-permute-start.1) | collective-permute-done | bytes 1056 | tf_op jit(solution)/shard_map/ppermute | solution.py:16
  18.9 0.0 collective-permute-done.earlier_texts
  18.9 0.0 copy-done.2
  18.9 0.0 collective-permute-start.3
  18.9 8.5 %shard_map.50 = (f32[32,1,128]{2,1,0:T(1,128)}, f32[256,1024]{1,0:T(8,128)}, f32[256,1024]{1,0:T(8,128)}, f32[256,1024]{1,0:T(8,128)}) custom-call(bf16[3,256,1024]{2,1,0:T(8,128)(2,1)S(1)} %get-tuple-element.30.image_parts, bf16[3,256,1024]{2,1,0:T(8,128)(2,1)S(1)} %get-tuple-element.31.text_parts, f32[256,1024]{1,0:T(8,128)S(1)} %collective-permute-done.earlier_texts, ...), custom_call_target="tpu_custom_call" | custom-call | flops 4026531840 | bytes 4194304 | tf_op jit(solution)/shard_map/pallas_call | solution.py:222
  27.4 0.0 copy-done
  27.4 3.7 %all-to-all-start = ((f32[32,1,128]{2,1,0:T(1,128)}), f32[32,1,128]{2,1,0:T(1,128)S(1)}, u32[]{:S(2)}, u32[]{:S(2)}) async-start(f32[32,1,128]{2,1,0:T(1,128)} %get-tuple-element.41), calls=%async_computation | async-start | bytes 32768 | tf_op jit(solution)/shard_map/all_to_all | solution.py:258
  31.1 0.1 collective-permute-done.3.later_images
  31.2 0.0 copy-start.1
  31.2 0.9 %copy-done.1 = f32[256,256]{1,0:T(8,128)S(1)} copy-done((f32[256,256]{1,0:T(8,128)S(1)}, f32[256,256]{1,0:T(8,128)}, u32[]{:S(2)}) %copy-start.1) | copy-done | bytes 262168
  32.2 6.2 %shard_map.51 = (bf16[256,1536]{1,0:T(8,128)(2,1)S(1)}, bf16[3,256,1024]{2,1,0:T(8,128)(2,1)S(1)}, f32[1,256]{1,0:T(1,128)S(1)}, f32[256,1024]{1,0:T(8,128)}) custom-call(bf16[3,256,1024]{2,1,0:T(8,128)(2,1)} %get-tuple-element.24.text_store, f32[256,1024]{1,0:T(8,128)S(1)} %collective-permute-done.3.later_images, f32[256,256]{1,0:T(8,128)S(1)} %copy-done.1, ...), custom_call_target="tpu_custom_call" | custom-call | flops 1610612736 | bytes 4194304 | tf_op jit(solution)/shard_map/pallas_call | solution.py:222
  38.4 0.0 all-to-all-done.messages
  38.4 3.9 %shard_map.52 = (f32[1,1]{1,0:T(1,128)}, f32[256,1024]{1,0:T(8,128)}) custom-call(bf16[256,1536]{1,0:T(8,128)(2,1)S(1)} %get-tuple-element.36.left, bf16[3,256,1024]{2,1,0:T(8,128)(2,1)S(1)} %get-tuple-element.37.later_parts, f32[1,256]{1,0:T(1,128)S(1)} %get-tuple-element.38.columns, f32[1,256]{1,0:T(1,128)S(1)} %get-tuple-element.25.self_columns, ...), custom_call_target="tpu_custom_call" | custom-call | flops 805306368 | bytes 4194304 | tf_op jit(solution)/shard_map/pallas_call | solution.py:222
Async XLA Ops:
  0.6 18.3 %copy-start.2 = (f32[1,1,256,1024]{3,2,1,0:T(8,128)S(1)}, f32[1,1,256,1024]{3,2,1,0:T(8,128)}, u32[]{:S(2)}) copy-start(f32[1,1,256,1024]{3,2,1,0:T(8,128)} %param.2) | copy-start | bytes 3145732
  0.6 18.3 %collective-permute-start = (f32[256,1024]{1,0:T(8,128)}, f32[256,1024]{1,0:T(8,128)S(1)}, u32[]{:S(2)}, u32[]{:S(2)}) collective-permute-start(f32[256,1024]{1,0:T(8,128)} %bitcast.5), channel_id=1, source_target_pairs={{0,2},{2,4},{4,6},{6,8},{8,10},{10,12},{12,14},{14,16},{16,18},{18... | collective-permute-start | bytes 3145736 | tf_op jit(solution)/shard_map/ppermute | solution.py:16
  5.2 22.2 %copy-start = (f32[256,256]{1,0:T(8,128)}, f32[256,256]{1,0:T(8,128)S(1)}, u32[]{:S(2)}) copy-start(f32[256,256]{1,0:T(8,128)S(1)} %get-tuple-element.28.logits) | copy-start | bytes 786436
  5.2 6.4 %collective-permute-start.2 = (f32[1,256]{1,0:T(1,128)S(1)}, f32[1,256]{1,0:T(1,128)S(1)}, u32[]{:S(2)}, u32[]{:S(2)}) collective-permute-start(f32[1,256]{1,0:T(1,128)S(1)} %get-tuple-element.26.self_rows), channel_id=1, source_target_pairs={{0,30},{2,0},{4,2},{6,4},{8,6},{10,8},{12,10},{14,12},{16,14},{18,... | collective-permute-start | bytes 3080 | tf_op jit(solution)/shard_map/ppermute | solution.py:16
  10.3 8.6 %collective-permute-start.1 = (f32[1,256]{1,0:T(1,128)S(1)}, f32[1,256]{1,0:T(1,128)S(1)}, u32[]{:S(2)}, u32[]{:S(2)}) collective-permute-start(f32[1,256]{1,0:T(1,128)S(1)} %get-tuple-element.25.self_columns), channel_id=1, source_target_pairs={{0,2},{2,4},{4,6},{6,8},{8,10},{10,12},{12,14},{14,16},{16,18},{18... | collective-permute-start | bytes 3080 | tf_op jit(solution)/shard_map/ppermute | solution.py:16
  18.9 12.3 %collective-permute-start.3 = (f32[256,1024]{1,0:T(8,128)S(1)}, f32[256,1024]{1,0:T(8,128)S(1)}, u32[]{:S(2)}, u32[]{:S(2)}) collective-permute-start(f32[256,1024]{1,0:T(8,128)S(1)} %bitcast.8), channel_id=1, source_target_pairs={{0,30},{2,0},{4,2},{6,4},{8,6},{10,8},{12,10},{14,12},{16,14},{18,... | collective-permute-start | bytes 3145736 | tf_op jit(solution)/shard_map/ppermute | solution.py:16
  27.4 11.0 %all-to-all-start = ((f32[32,1,128]{2,1,0:T(1,128)}), f32[32,1,128]{2,1,0:T(1,128)S(1)}, u32[]{:S(2)}, u32[]{:S(2)}) async-start(f32[32,1,128]{2,1,0:T(1,128)} %get-tuple-element.41), calls=%async_computation | async-start | bytes 32768 | tf_op jit(solution)/shard_map/all_to_all | solution.py:258
  31.2 0.9 %copy-start.1 = (f32[256,256]{1,0:T(8,128)S(1)}, f32[256,256]{1,0:T(8,128)}, u32[]{:S(2)}) copy-start(f32[256,256]{1,0:T(8,128)} %copy-done) | copy-start | bytes 786436

commit v2 on v1

v2 whole, which is shorter than its diff:
```python
import functools

import jax
import jax.numpy as jnp
from jax import lax
from jax.experimental import pallas as pl
from jax.experimental.pallas import tpu as pltpu
from jax.sharding import PartitionSpec as P

logit_scale = 0.03125
f32, bf16 = jnp.float32, jnp.bfloat16
LANES = 128


def from_behind(value, axis, steps):
    count = lax.axis_size(axis)
    pairs = [(source, (source + steps) % count) for source in range(count)]
    return lax.ppermute(value, axis, pairs)


def split(value):
    high = value.astype(bf16)
    rest = value - high.astype(f32)
    middle = rest.astype(bf16)
    low = (rest - middle.astype(f32)).astype(bf16)
    return high, middle, low


PAIRS = ((2, 0), (1, 1), (0, 2), (1, 0), (0, 1), (0, 0))


def rows_by_rows(left, right):
    return lax.dot_general(
        jnp.concatenate([left[one] for one, _ in PAIRS], axis=1),
        jnp.concatenate([right[other] for _, other in PAIRS], axis=1),
        (((1,), (1,)), ((), ())),
        preferred_element_type=f32,
    )


def left_parts(left):
    parts = split(left)
    return jnp.concatenate([parts[one] for one, _ in PAIRS], axis=1)


def rows_by_columns(left, right):
    return jnp.dot(left, jnp.concatenate([right[other] for _, other in PAIRS], axis=0), preferred_element_type=f32)


def store_parts(stacked, value):
    for place, part in enumerate(split(value)):
        stacked[place] = part


def logsum(logits, axis):
    largest = jnp.max(logits, axis=axis, keepdims=True)
    return largest + jnp.log(jnp.sum(jnp.exp(logits - largest), axis=axis, keepdims=True))


def paired_logsum(former, latter):
    largest = jnp.maximum(former, latter)
    return largest + jnp.log(jnp.exp(former - largest) + jnp.exp(latter - largest))


def diagonal_mask(count):
    shape = (count, count)
    return lax.broadcasted_iota(jnp.int32, shape, 0) == lax.broadcasted_iota(jnp.int32, shape, 1)


def as_row(column, diagonal):
    return jnp.sum(jnp.where(diagonal, column, 0.0), axis=0, keepdims=True)


def as_column(row, diagonal):
    return jnp.sum(jnp.where(diagonal, row, 0.0), axis=1, keepdims=True)


def total(values):
    return jnp.sum(jnp.sum(values, axis=1, keepdims=True), axis=0, keepdims=True)


def start(pairs, semaphores):
    copies = [pltpu.make_async_copy(source, target, semaphores.at[k]) for k, (source, target) in enumerate(pairs)]
    for copy in copies:
        copy.start()
    return copies


def columns_at(k, size):
    return pl.ds(pl.multiple_of(k * size, size), size)


def self_kernel(
    images, texts,
    logits, image_parts, row_part, positive, column_part, image_store, text_store, row_product, column_term,
    image_in, text_in, text_parts, left, down, row_out, column_out, semaphores,
):
    copies = start([(images, image_in), (texts, text_in)], semaphores)
    copies[0].wait()
    store_parts(image_parts, image_in[...])
    copies[1].wait()
    store_parts(text_parts, text_in[...])
    copies = start([(image_parts, image_store), (text_parts, text_store)], semaphores)
    block = logit_scale * rows_by_rows(image_parts, text_parts)
    count, width = text_in.shape
    diagonal = diagonal_mask(count)
    rows, columns = logsum(block, 1), logsum(block, 0)
    logits[...] = block
    row_part[...] = as_row(rows, diagonal)
    column_part[...] = columns
    positive[...] = total(jnp.where(diagonal, block, 0.0))
    left[...] = left_parts(0.5 * jnp.exp(block - rows))
    down[...] = left_parts((0.5 * jnp.exp(block - columns)).T)
    half = width // 2

    @pl.loop(0, 2)
    def _(k):
        part = columns_at(k, half)
        row_out[:, part] = rows_by_columns(left[...], text_parts.at[:, :, part])
        column_out[:, part] = rows_by_columns(down[...], image_parts.at[:, :, part])

    copies += start([(row_out, row_product), (column_out, column_term)], semaphores.at[2:4])
    for copy in copies:
        copy.wait()


def earlier_kernel(
    image_parts, earlier_texts, self_rows, before_columns, positive,
    messages, weights, rows_out,
):
    block = logit_scale * rows_by_rows(image_parts, split(earlier_texts[...]))
    diagonal = diagonal_mask(block.shape[0])
    rows = paired_logsum(as_column(self_rows[...], diagonal), logsum(block, 1))
    columns = paired_logsum(before_columns[...], logsum(block, 0))
    messages[...] = jnp.broadcast_to(0.5 * (total(rows) + total(columns)) - positive[...], messages.shape)
    weights[...] = 0.5 * (jnp.exp(block - rows) + jnp.exp(block - columns))
    rows_out[...] = as_row(rows, diagonal)


def middle_kernel(
    weights, earlier_texts, rows, logits, self_rows, image_store, text_store, row_store,
    image_part, row_term, text_parts,
    earlier_parts, image_parts, row_product, left, down, semaphores,
):
    copies = start([(text_store, text_parts), (row_store, row_product), (image_store, image_parts)], semaphores)
    count, width = image_part.shape
    diagonal = diagonal_mask(count)
    left[...] = left_parts(weights[...])
    store_parts(earlier_parts, earlier_texts[...])
    joint = as_column(rows[...], diagonal)
    down[...] = left_parts((0.5 * jnp.exp(logits[...] - joint) - jnp.where(diagonal, 1.0, 0.0)).T)
    scale = as_column(jnp.exp(self_rows[...] - rows[...]), diagonal)
    half = width // 2
    copies[0].wait()
    copies[1].wait()

    @pl.loop(0, 2)
    def _(k):
        part = columns_at(k, half)
        own = text_parts[0, :, part].astype(f32) + text_parts[1, :, part].astype(f32) + text_parts[2, :, part].astype(f32)
        terms = rows_by_columns(left[...], earlier_parts.at[:, :, part])
        image_part[:, part] = terms + scale * row_product[:, part] - own

    copies[2].wait()

    @pl.loop(0, 2)
    def _(k):
        part = columns_at(k, half)
        row_term[:, part] = rows_by_columns(down[...], image_parts.at[:, :, part])


def last_kernel(
    text_parts, later_images, logits, later_rows, self_columns, image_part, row_term, column_term,
    image_grads, text_grads,
    later_parts, left, own_left, column_in, image_out, text_out, semaphores,
):
    (column_copy,) = start([(column_term, column_in)], semaphores.at[4:5])
    count, width = image_out.shape
    diagonal = diagonal_mask(count)
    store_parts(later_parts, later_images[...])
    block = logit_scale * rows_by_rows(text_parts, later_parts)
    rows = paired_logsum(later_rows[...], logsum(block, 0))
    own_columns = as_column(self_columns[...], diagonal)
    columns = paired_logsum(own_columns, logsum(block, 1))
    left[...] = left_parts(0.5 * (jnp.exp(block - rows) + jnp.exp(block - columns)))
    own_left[...] = left_parts(0.5 * jnp.exp(logits[...] - as_row(columns, diagonal)))
    scale = jnp.exp(own_columns - columns)
    half = width // 2
    column_copy.wait()

    def copies(k):
        part = columns_at(k, half)
        return (
            pltpu.make_async_copy(image_out.at[:, part], image_grads.at[:, part], semaphores.at[2 * k]),
            pltpu.make_async_copy(text_out.at[:, part], text_grads.at[:, part], semaphores.at[2 * k + 1]),
        )

    @pl.loop(0, 2)
    def _(k):
        part = columns_at(k, half)
        of_image, of_text = copies(k)
        terms = rows_by_columns(own_left[...], text_parts.at[:, :, part])
        image_out[:, part] = logit_scale * (image_part[:, part] + terms)
        of_image.start()
        terms = rows_by_columns(left[...], later_parts.at[:, :, part])
        text_out[:, part] = logit_scale * (row_term[:, part] + scale * column_in[:, part] + terms)
        of_text.start()

    for k in range(2):
        for copy in copies(k):
            copy.wait()


def loss_kernel(messages, mean_loss, *, rows):
    mean_loss[...] = total(messages[:, 0, 0:1]) / rows


VM, HB, SM = pl.BlockSpec(memory_space=pltpu.VMEM), pl.BlockSpec(memory_space=pltpu.HBM), pl.BlockSpec(memory_space=pltpu.SMEM)


def call(kernel, products, ins, outs, scratch, copies):
    def shape_of(place, shape, dtype):
        if place is HB:
            return pltpu.HBM(shape, dtype)
        return jax.ShapeDtypeStruct(shape, dtype)

    run = pl.pallas_call(
        kernel,
        out_shape=[shape_of(*out) for out in outs],
        in_specs=ins,
        out_specs=[out[0] for out in outs],
        scratch_shapes=[pltpu.VMEM(shape, dtype) for shape, dtype in scratch]
        + ([pltpu.SemaphoreType.DMA((copies,))] if copies else []),
        compiler_params=pltpu.CompilerParams(vmem_limit_bytes=28 << 20),
        cost_estimate=pl.CostEstimate(
            flops=products * 12 * 256 * 256 * 1024, bytes_accessed=4 << 20, transcendentals=1 << 18
        ),
    )

    def pinned(*values):
        return run(
            *[pltpu.with_memory_space_constraint(v, pltpu.HBM) if spec is HB else v for v, spec in zip(values, ins)]
        )

    return pinned


def on_device(image_embeds, text_embeds):
    images, texts = image_embeds[0, 0], text_embeds[0, 0]
    count, width = images.shape
    square, row, whole = ((count, count), f32), ((1, count), f32), ((count, width), f32)
    parts, left = ((3, count, width), bf16), ((count, len(PAIRS) * count), bf16)
    devices = lax.axis_size("dp") * lax.axis_size("hst")
    earlier_texts = from_behind(texts, "dp", 1)
    (
        logits, image_parts, self_rows, positive, self_columns, image_store, text_store, row_product, column_term
    ) = call(
        self_kernel,
        3,
        [HB, HB],
        [
            (VM, *square), (VM, *parts), (VM, *row), (VM, (1, 1), f32), (VM, *row),
            (HB, *parts), (HB, *parts), (HB, *whole), (HB, *whole),
        ],
        [whole, whole, parts, left, left, whole, whole],
        4,
    )(images, texts)
    before_columns = from_behind(self_columns, "dp", 1)
    later_rows = from_behind(self_rows, "dp", -1)
    earlier_texts, images, before_columns, later_rows, image_parts = lax.optimization_barrier(
        (earlier_texts, images, before_columns, later_rows, image_parts)
    )
    later_images = from_behind(images, "dp", -1)
    messages, weights, rows = call(
        earlier_kernel,
        1,
        [VM] * 5,
        [(VM, (devices, 1, LANES), f32), (VM, *square), (VM, *row)],
        [],
        0,
    )(image_parts, earlier_texts, self_rows, before_columns, positive)
    messages = lax.all_to_all(messages, ("dp", "hst"), 0, 0, tiled=True)
    image_part, row_term, text_parts = call(
        middle_kernel,
        2,
        [VM] * 5 + [HB] * 3,
        [(VM, *whole), (VM, *whole), (VM, *parts)],
        [parts, parts, whole, left, left],
        3,
    )(weights, earlier_texts, rows, logits, self_rows, image_store, text_store, row_product)
    image_grads, text_grads = call(
        last_kernel,
        3,
        [VM] * 7 + [HB],
        [(HB, *whole), (HB, *whole)],
        [parts, left, left, whole, whole, whole],
        5,
    )(text_parts, later_images, logits, later_rows, self_columns, image_part, row_term, column_term)
    messages, text_grads = lax.optimization_barrier((messages, text_grads))
    (mean_loss,) = call(functools.partial(loss_kernel, rows=count * devices), 0, [VM], [(VM, (1, 1), f32)], [], 0)(messages)
    return mean_loss[0, 0], image_grads[None, None], text_grads[None, None]


def solution(mesh):
    return jax.shard_map(
        on_device,
        mesh=mesh,
        in_specs=(P("dp", "hst", None, None), P("dp", "hst", None, None)),
        out_specs=(P(), P("dp", "hst", None, None), P("dp", "hst", None, None)),
        check_vma=False,
    )
```

time: 42.6 us -> 36.8 us (0.86)
  Pallas kernels: 22.7 us -> 18.1 us
  local copies, waits for them, and re-layouts: 0.96 us -> 0 us
    pallas_call x4 -> x5, Pallas kernels: 22.7 us -> 18.1 us  [pinned(): run(*[pltpu.with_memory_space_constraint(v, pltpu.HBM) if spec is HB else...]
    unnamed x6 -> x0, local copies, waits for them, and re-layouts: 0.96 us -> none
  transfers between devices with their start and end apart: 5 -> 5, of which waited for: 3 -> 2; matrix products, arithmetic and copies ran while one was open for 0% -> 0% of each run, Pallas kernels for 44% -> 48%
where the time goes in v2:
time: 36.8 us; the launch traced here: 36.7 us
  Pallas kernels  18.1 us (49%)
  starting transfers between devices  9.34 us (25%)
  waiting for transfers between devices  8.58 us (23%)
  between operations  0.68 us (2%)
    pallas_call x5, Pallas kernels, pinned(): run(*[pltpu.with_memory_space_constraint(v, pltpu.HBM) if spec is HB else...  18.1 us
    ppermute x4, waiting for transfers between devices, from_behind(): return lax.ppermute(value, axis, pairs)  8.57 us
    ppermute x4, starting transfers between devices, from_behind(): return lax.ppermute(value, axis, pairs)  5.64 us
    all_to_all x1, starting transfers between devices, on_device(): messages = lax.all_to_all(messages, ('dp', 'hst'), 0, 0, tiled=True)  3.7 us
  transfers between devices with their start and end apart: 5, of which 2 were waited for; matrix products, arithmetic and copies ran while one was open for 0% of the time, Pallas kernels for 48%

profile of v2, /device:TPU:0, one launch (start us, length us, event | category | flops | bytes accessed | tf_op | source)
XLA Modules:
  0.0 36.7 jit_solution(18243697329125419044)
XLA Ops:
  0.6 0.5 %collective-permute-start = (f32[256,1024]{1,0:T(8,128)}, f32[256,1024]{1,0:T(8,128)S(1)}, u32[]{:S(2)}, u32[]{:S(2)}) collective-permute-start(f32[256,1024]{1,0:T(8,128)} %bitcast.5), channel_id=1, source_target_pairs={{0,2},{2,4},{4,6},{6,8},{8,10},{10,12},{12,14},{14,16},{16,18},{18... | collective-permute-start | bytes 3145736 | tf_op jit(solution)/shard_map/ppermute | solution.py:18
  1.1 6.4 %shard_map.49 = (f32[256,256]{1,0:T(8,128)S(1)}, bf16[3,256,1024]{2,1,0:T(8,128)(2,1)S(1)}, f32[1,256]{1,0:T(1,128)S(1)}, f32[1,1]{1,0:T(1,128)}, f32[1,256]{1,0...) custom-call(f32[256,1024]{1,0:T(8,128)} %bitcast.1.images, ...), custom_call_target="tpu_custom_call" | custom-call | flops 2415919104 | bytes 4194304 | tf_op jit(solution)/shard_map/pallas_call | solution.py:241
  7.6 2.7 %collective-permute-start.1 = (f32[1,256]{1,0:T(1,128)S(1)}, f32[1,256]{1,0:T(1,128)S(1)}, u32[]{:S(2)}, u32[]{:S(2)}) collective-permute-start(f32[1,256]{1,0:T(1,128)S(1)} %get-tuple-element.27.self_columns), channel_id=1, source_target_pairs={{0,2},{2,4},{4,6},{6,8},{8,10},{10,12},{12,14},{14,16},{16,18},{18... | collective-permute-start | bytes 3080 | tf_op jit(solution)/shard_map/ppermute | solution.py:18
  10.2 2.4 %collective-permute-start.2 = (f32[1,256]{1,0:T(1,128)S(1)}, f32[1,256]{1,0:T(1,128)S(1)}, u32[]{:S(2)}, u32[]{:S(2)}) collective-permute-start(f32[1,256]{1,0:T(1,128)S(1)} %get-tuple-element.28.self_rows), channel_id=1, source_target_pairs={{0,30},{2,0},{4,2},{6,4},{8,6},{10,8},{12,10},{14,12},{16,14},{18,... | collective-permute-start | bytes 3080 | tf_op jit(solution)/shard_map/ppermute | solution.py:18
  12.7 6.2 %collective-permute-done.1.before_columns = f32[1,256]{1,0:T(1,128)S(1)} collective-permute-done((f32[1,256]{1,0:T(1,128)S(1)}, f32[1,256]{1,0:T(1,128)S(1)}, u32[]{:S(2)}, u32[]{:S(2)}) %collective-permute-start.1) | collective-permute-done | bytes 1056 | tf_op jit(solution)/shard_map/ppermute | solution.py:18
  18.9 0.0 collective-permute-done.2.later_rows
  18.9 0.0 collective-permute-done.earlier_texts
  18.9 0.0 collective-permute-start.3
  18.9 2.6 %shard_map.50 = (f32[32,1,128]{2,1,0:T(1,128)}, f32[256,256]{1,0:T(8,128)S(1)}, f32[1,256]{1,0:T(1,128)S(1)}) custom-call(bf16[3,256,1024]{2,1,0:T(8,128)(2,1)S(1)} %get-tuple-element.30.image_parts, f32[256,1024]{1,0:T(8,128)S(1)} %collective-permute-done.earlier_texts, f32[1,256]{1,0:T(1,128)S(1)} %get-tuple-element.28.self_rows, ...), custom_call_target="tpu_custom_call" | custom-call | flops 805306368 | bytes 4194304 | tf_op jit(solution)/shard_map/pallas_call | solution.py:241
  21.5 3.7 %all-to-all-start = ((f32[32,1,128]{2,1,0:T(1,128)}), f32[32,1,128]{2,1,0:T(1,128)S(1)}, u32[]{:S(2)}, u32[]{:S(2)}) async-start(f32[32,1,128]{2,1,0:T(1,128)} %get-tuple-element.34), calls=%async_computation | async-start | bytes 32768 | tf_op jit(solution)/shard_map/all_to_all | solution.py:282
  25.2 4.1 %shard_map.51 = (f32[256,1024]{1,0:T(8,128)S(1)}, f32[256,1024]{1,0:T(8,128)S(1)}, bf16[3,256,1024]{2,1,0:T(8,128)(2,1)S(1)}) custom-call(f32[256,256]{1,0:T(8,128)S(1)} %get-tuple-element.35.weights, f32[256,1024]{1,0:T(8,128)S(1)} %collective-permute-done.earlier_texts, f32[1,256]{1,0:T(1,128)S(1)} %get-tuple-element.36.rows, ...), custom_call_target="tpu_custom_call" | custom-call | flops 1610612736 | bytes 4194304 | tf_op jit(solution)/shard_map/pallas_call | solution.py:241
  29.3 2.4 %collective-permute-done.3.later_images = f32[256,1024]{1,0:T(8,128)S(1)} collective-permute-done((f32[256,1024]{1,0:T(8,128)}, f32[256,1024]{1,0:T(8,128)S(1)}, u32[]{:S(2)}, u32[]{:S(2)}) %collective-permute-start.3) | collective-permute-done | bytes 1048608 | tf_op jit(solution)/shard_map/ppermute | solution.py:18
  31.7 4.4 %shard_map.52 = (f32[256,1024]{1,0:T(8,128)}, f32[256,1024]{1,0:T(8,128)}) custom-call(bf16[3,256,1024]{2,1,0:T(8,128)(2,1)S(1)} %get-tuple-element.41.text_parts, f32[256,1024]{1,0:T(8,128)S(1)} %collective-permute-done.3.later_images, f32[256,256]{1,0:T(8,128)S(1)} %get-tuple-element.37.logits, f32[1,256]{1,0:T(1,128)S(1)} %collective-permute-done.2.later_rows, ...), custom_call_target="tpu_custom_call" | custom-call | flops 2415919104 | bytes 4194304 | tf_op jit(solution)/shard_map/pallas_call | solution.py:241
  36.1 0.0 all-to-all-done.messages
  36.1 0.5 %shard_map.53 = f32[1,1]{1,0:T(1,128)} custom-call(f32[32,1,128]{2,1,0:T(1,128)S(1)} %all-to-all-done.messages), custom_call_target="tpu_custom_call" | custom-call | bytes 4194304 | tf_op jit(solution)/shard_map/pallas_call | solution.py:241
Async XLA Ops:
  0.6 18.3 %collective-permute-start = (f32[256,1024]{1,0:T(8,128)}, f32[256,1024]{1,0:T(8,128)S(1)}, u32[]{:S(2)}, u32[]{:S(2)}) collective-permute-start(f32[256,1024]{1,0:T(8,128)} %bitcast.5), channel_id=1, source_target_pairs={{0,2},{2,4},{4,6},{6,8},{8,10},{10,12},{12,14},{14,16},{16,18},{18... | collective-permute-start | bytes 3145736 | tf_op jit(solution)/shard_map/ppermute | solution.py:18
  7.6 11.3 %collective-permute-start.1 = (f32[1,256]{1,0:T(1,128)S(1)}, f32[1,256]{1,0:T(1,128)S(1)}, u32[]{:S(2)}, u32[]{:S(2)}) collective-permute-start(f32[1,256]{1,0:T(1,128)S(1)} %get-tuple-element.27.self_columns), channel_id=1, source_target_pairs={{0,2},{2,4},{4,6},{6,8},{8,10},{10,12},{12,14},{14,16},{16,18},{18... | collective-permute-start | bytes 3080 | tf_op jit(solution)/shard_map/ppermute | solution.py:18
  10.2 8.6 %collective-permute-start.2 = (f32[1,256]{1,0:T(1,128)S(1)}, f32[1,256]{1,0:T(1,128)S(1)}, u32[]{:S(2)}, u32[]{:S(2)}) collective-permute-start(f32[1,256]{1,0:T(1,128)S(1)} %get-tuple-element.28.self_rows), channel_id=1, source_target_pairs={{0,30},{2,0},{4,2},{6,4},{8,6},{10,8},{12,10},{14,12},{16,14},{18,... | collective-permute-start | bytes 3080 | tf_op jit(solution)/shard_map/ppermute | solution.py:18
  18.9 12.8 %collective-permute-start.3 = (f32[256,1024]{1,0:T(8,128)}, f32[256,1024]{1,0:T(8,128)S(1)}, u32[]{:S(2)}, u32[]{:S(2)}) collective-permute-start(f32[256,1024]{1,0:T(8,128)} %bitcast.1.images), channel_id=1, source_target_pairs={{0,30},{2,0},{4,2},{6,4},{8,6},{10,8},{12,10},{14,12},{16,14},{18,... | collective-permute-start | bytes 3145736 | tf_op jit(solution)/shard_map/ppermute | solution.py:18
  21.5 14.6 %all-to-all-start = ((f32[32,1,128]{2,1,0:T(1,128)}), f32[32,1,128]{2,1,0:T(1,128)S(1)}, u32[]{:S(2)}, u32[]{:S(2)}) async-start(f32[32,1,128]{2,1,0:T(1,128)} %get-tuple-element.34), calls=%async_computation | async-start | bytes 32768 | tf_op jit(solution)/shard_map/all_to_all | solution.py:282

commit v3 on v2

--- a/solution.py
+++ b/solution.py
@@ -92,8 +92,8 @@
 
 def self_kernel(
     images, texts,
-    logits, image_parts, row_part, positive, column_part, image_store, text_store, row_product, column_term,
-    image_in, text_in, text_parts, left, down, row_out, column_out, semaphores,
+    image_parts, row_part, positive, column_part, logits, image_store, text_store, row_product, column_term,
+    own, image_in, text_in, text_parts, left, down, row_out, column_out, semaphores,
 ):
     copies = start([(images, image_in), (texts, text_in)], semaphores)
     copies[0].wait()
@@ -105,10 +105,10 @@
     count, width = text_in.shape
     diagonal = diagonal_mask(count)
     rows, columns = logsum(block, 1), logsum(block, 0)
-    logits[...] = block
+    own[...] = block
     row_part[...] = as_row(rows, diagonal)
     column_part[...] = columns
-    positive[...] = total(jnp.where(diagonal, block, 0.0))
+    positive[...] = as_row(block, diagonal)
     left[...] = left_parts(0.5 * jnp.exp(block - rows))
     down[...] = left_parts((0.5 * jnp.exp(block - columns)).T)
     half = width // 2
@@ -119,7 +119,7 @@
         row_out[:, part] = rows_by_columns(left[...], text_parts.at[:, :, part])
         column_out[:, part] = rows_by_columns(down[...], image_parts.at[:, :, part])
 
-    copies += start([(row_out, row_product), (column_out, column_term)], semaphores.at[2:4])
+    copies += start([(row_out, row_product), (column_out, column_term), (own, logits)], semaphores.at[2:5])
     for copy in copies:
         copy.wait()
 
@@ -130,55 +130,68 @@
 ):
     block = logit_scale * rows_by_rows(image_parts, split(earlier_texts[...]))
     diagonal = diagonal_mask(block.shape[0])
-    rows = paired_logsum(as_column(self_rows[...], diagonal), logsum(block, 1))
+    rows = paired_logsum(self_rows[...], as_row(logsum(block, 1), diagonal))
     columns = paired_logsum(before_columns[...], logsum(block, 0))
-    messages[...] = jnp.broadcast_to(0.5 * (total(rows) + total(columns)) - positive[...], messages.shape)
-    weights[...] = 0.5 * (jnp.exp(block - rows) + jnp.exp(block - columns))
-    rows_out[...] = as_row(rows, diagonal)
+    partial = jnp.sum(0.5 * (rows + columns) - positive[...], axis=1, keepdims=True)
+    messages[...] = jnp.broadcast_to(partial, messages.shape)
+    weights[...] = 0.5 * (jnp.exp(block - as_column(rows, diagonal)) + jnp.exp(block - columns))
+    rows_out[...] = rows
 
 
 def middle_kernel(
-    weights, earlier_texts, rows, logits, self_rows, image_store, text_store, row_store,
-    image_part, row_term, text_parts,
+    weights, earlier_texts, rows, self_rows, logits, image_store, text_store, row_store,
+    image_part, row_term, text_parts, own,
     earlier_parts, image_parts, row_product, left, down, semaphores,
 ):
-    copies = start([(text_store, text_parts), (row_store, row_product), (image_store, image_parts)], semaphores)
+    copies = start(
+        [(logits, own), (image_store, image_parts), (row_store, row_product), (text_store, text_parts)], semaphores
+    )
     count, width = image_part.shape
     diagonal = diagonal_mask(count)
     left[...] = left_parts(weights[...])
     store_parts(earlier_parts, earlier_texts[...])
     joint = as_column(rows[...], diagonal)
-    down[...] = left_parts((0.5 * jnp.exp(logits[...] - joint) - jnp.where(diagonal, 1.0, 0.0)).T)
     scale = as_column(jnp.exp(self_rows[...] - rows[...]), diagonal)
     half = width // 2
-    copies[0].wait()
-    copies[1].wait()
 
     @pl.loop(0, 2)
     def _(k):
         part = columns_at(k, half)
-        own = text_parts[0, :, part].astype(f32) + text_parts[1, :, part].astype(f32) + text_parts[2, :, part].astype(f32)
-        terms = rows_by_columns(left[...], earlier_parts.at[:, :, part])
-        image_part[:, part] = terms + scale * row_product[:, part] - own
-
-    copies[2].wait()
+        image_part[:, part] = rows_by_columns(left[...], earlier_parts.at[:, :, part])
+
+    copies[0].wait()
+    down[...] = left_parts((0.5 * jnp.exp(own[...] - joint) - jnp.where(diagonal, 1.0, 0.0)).T)
+    copies[1].wait()
 
     @pl.loop(0, 2)
     def _(k):
         part = columns_at(k, half)
         row_term[:, part] = rows_by_columns(down[...], image_parts.at[:, :, part])
 
+    copies[2].wait()
+    copies[3].wait()
+    whole = text_parts[0].astype(f32) + text_parts[1].astype(f32) + text_parts[2].astype(f32)
+    image_part[...] += scale * row_product[...] - whole
+
+
+def first_kernel(text_parts, first, column_store, later_parts, product, column_term, semaphores):
+    (copy,) = start([(column_store, column_term)], semaphores)
+    part = slice(0, first.shape[1])
+    store_parts(later_parts.at[:, :, part], first[...])
+    product[...] = rows_by_rows(text_parts.at[:, :, part], later_parts.at[:, :, part])
+    copy.wait()
+
 
 def last_kernel(
-    text_parts, later_images, logits, later_rows, self_columns, image_part, row_term, column_term,
-    image_grads, text_grads,
-    later_parts, left, own_left, column_in, image_out, text_out, semaphores,
+    text_parts, first_parts, second, product, logits, later_rows, self_columns, image_part, row_term, column_term,
+    later_parts, image_grads, text_grads,
+    left, own_left, image_out, text_out, semaphores,
 ):
-    (column_copy,) = start([(column_term, column_in)], semaphores.at[4:5])
     count, width = image_out.shape
     diagonal = diagonal_mask(count)
-    store_parts(later_parts, later_images[...])
-    block = logit_scale * rows_by_rows(text_parts, later_parts)
+    part = slice(width - second.shape[1], width)
+    store_parts(later_parts.at[:, :, part], second[...])
+    block = logit_scale * (product[...] + rows_by_rows(text_parts.at[:, :, part], later_parts.at[:, :, part]))
     rows = paired_logsum(later_rows[...], logsum(block, 0))
     own_columns = as_column(self_columns[...], diagonal)
     columns = paired_logsum(own_columns, logsum(block, 1))
@@ -186,7 +199,6 @@
     own_left[...] = left_parts(0.5 * jnp.exp(logits[...] - as_row(columns, diagonal)))
     scale = jnp.exp(own_columns - columns)
     half = width // 2
-    column_copy.wait()
 
     def copies(k):
         part = columns_at(k, half)
@@ -203,7 +215,7 @@
         image_out[:, part] = logit_scale * (image_part[:, part] + terms)
         of_image.start()
         terms = rows_by_columns(left[...], later_parts.at[:, :, part])
-        text_out[:, part] = logit_scale * (row_term[:, part] + scale * column_in[:, part] + terms)
+        text_out[:, part] = logit_scale * (row_term[:, part] + scale * column_term[:, part] + terms)
         of_text.start()
 
     for k in range(2):
@@ -215,19 +227,22 @@
     mean_loss[...] = total(messages[:, 0, 0:1]) / rows
 
 
-VM, HB, SM = pl.BlockSpec(memory_space=pltpu.VMEM), pl.BlockSpec(memory_space=pltpu.HBM), pl.BlockSpec(memory_space=pltpu.SMEM)
-
-
-def call(kernel, products, ins, outs, scratch, copies):
+VM, PV, HB = (pl.BlockSpec(memory_space=place) for place in (pltpu.VMEM, pltpu.VMEM, pltpu.HBM))
+
+
+def call(kernel, products, ins, outs, scratch, copies, aliases=None):
     def shape_of(place, shape, dtype):
         if place is HB:
             return pltpu.HBM(shape, dtype)
+        if place is PV:
+            return pltpu.VMEM(shape, dtype)
         return jax.ShapeDtypeStruct(shape, dtype)
 
     run = pl.pallas_call(
         kernel,
         out_shape=[shape_of(*out) for out in outs],
         in_specs=ins,
+        input_output_aliases=aliases or {},
         out_specs=[out[0] for out in outs],
         scratch_shapes=[pltpu.VMEM(shape, dtype) for shape, dtype in scratch]
         + ([pltpu.SemaphoreType.DMA((copies,))] if copies else []),
@@ -248,54 +263,61 @@
 def on_device(image_embeds, text_embeds):
     images, texts = image_embeds[0, 0], text_embeds[0, 0]
     count, width = images.shape
+    small = width // 4
     square, row, whole = ((count, count), f32), ((1, count), f32), ((count, width), f32)
     parts, left = ((3, count, width), bf16), ((count, len(PAIRS) * count), bf16)
     devices = lax.axis_size("dp") * lax.axis_size("hst")
     earlier_texts = from_behind(texts, "dp", 1)
     (
-        logits, image_parts, self_rows, positive, self_columns, image_store, text_store, row_product, column_term
+        image_parts, self_rows, positive, self_columns, logits, image_store, text_store, row_product, column_term
     ) = call(
         self_kernel,
         3,
         [HB, HB],
         [
-            (VM, *square), (VM, *parts), (VM, *row), (VM, (1, 1), f32), (VM, *row),
-            (HB, *parts), (HB, *parts), (HB, *whole), (HB, *whole),
+            (VM, *parts), (VM, *row), (VM, *row), (VM, *row),
+            (HB, *square), (HB, *parts), (HB, *parts), (HB, *whole), (HB, *whole),
         ],
-        [whole, whole, parts, left, left, whole, whole],
-        4,
+        [square, whole, whole, parts, left, left, whole, whole],
+        5,
     )(images, texts)
     before_columns = from_behind(self_columns, "dp", 1)
     later_rows = from_behind(self_rows, "dp", -1)
-    earlier_texts, images, before_columns, later_rows, image_parts = lax.optimization_barrier(
-        (earlier_texts, images, before_columns, later_rows, image_parts)
-    )
-    later_images = from_behind(images, "dp", -1)
+    first, second = images[:, : width - small], images[:, width - small :]
+    earlier_texts, first, second, before_columns, later_rows, image_parts = lax.optimization_barrier(
+        (earlier_texts, first, second, before_columns, later_rows, image_parts)
+    )
+    first = from_behind(first, "dp", -1)
+    second = from_behind(second, "dp", -1)
     messages, weights, rows = call(
         earlier_kernel,
         1,
         [VM] * 5,
-        [(VM, (devices, 1, LANES), f32), (VM, *square), (VM, *row)],
+        [(PV, (devices, 1, LANES), f32), (VM, *square), (VM, *row)],
         [],
         0,
     )(image_parts, earlier_texts, self_rows, before_columns, positive)
     messages = lax.all_to_all(messages, ("dp", "hst"), 0, 0, tiled=True)
-    image_part, row_term, text_parts = call(
+    image_part, row_term, text_parts, logits = call(
         middle_kernel,
         2,
-        [VM] * 5 + [HB] * 3,
-        [(VM, *whole), (VM, *whole), (VM, *parts)],
+        [VM] * 4 + [HB] * 4,
+        [(VM, *whole), (VM, *whole), (VM, *parts), (VM, *square)],
         [parts, parts, whole, left, left],
-        3,
-    )(weights, earlier_texts, rows, logits, self_rows, image_store, text_store, row_product)
-    image_grads, text_grads = call(
+        4,
+    )(weights, earlier_texts, rows, self_rows, logits, image_store, text_store, row_product)
+    later_parts, product, column_term = call(
+        first_kernel, 1, [VM, VM, HB], [(VM, *parts), (VM, *square), (VM, *whole)], [], 1
+    )(text_parts, first, column_term)
+    _, image_grads, text_grads = call(
         last_kernel,
         3,
-        [VM] * 7 + [HB],
-        [(HB, *whole), (HB, *whole)],
-        [parts, left, left, whole, whole, whole],
-        5,
-    )(text_parts, later_images, logits, later_rows, self_columns, image_part, row_term, column_term)
+        [VM] * 10,
+        [(VM, *parts), (HB, *whole), (HB, *whole)],
+        [left, left, whole, whole],
+        4,
+        {1: 0},
+    )(text_parts, later_parts, second, product, logits, later_rows, self_columns, image_part, row_term, column_term)
     messages, text_grads = lax.optimization_barrier((messages, text_grads))
     (mean_loss,) = call(functools.partial(loss_kernel, rows=count * devices), 0, [VM], [(VM, (1, 1), f32)], [], 0)(messages)
     return mean_loss[0, 0], image_grads[None, None], text_grads[None, None]

time: 36.8 us -> 35.9 us (0.976)
  waiting for transfers between devices: 8.58 us -> 7.1 us
  starting transfers between devices: 9.34 us -> 10.7 us
  Pallas kernels: 18.1 us -> 17 us
    ppermute x4 -> x5, starting transfers between devices: 5.64 us -> 8.05 us  [from_behind(): return lax.ppermute(value, axis, pairs)]
    ppermute x4 -> x5, waiting for transfers between devices: 8.57 us -> 7.1 us  [from_behind(): return lax.ppermute(value, axis, pairs)]
    pallas_call x5 -> x6, Pallas kernels: 18.1 us -> 17 us  [pinned(): run(*[pltpu.with_memory_space_constraint(v, pltpu.HBM) if spec is HB else...]
    all_to_all x1, starting transfers between devices: 3.7 us -> 2.7 us  [on_device(): messages = lax.all_to_all(messages, ('dp', 'hst'), 0, 0, tiled=True)]
  transfers between devices with their start and end apart: 5 -> 6, of which waited for: 2 -> 2; matrix products, arithmetic and copies ran while one was open for 0% -> 0% of each run, Pallas kernels for 48% -> 46%
where the time goes in v3:
time: 35.9 us; the launch traced here: 35.7 us
  Pallas kernels  17 us (47%)
  starting transfers between devices  10.7 us (30%)
  waiting for transfers between devices  7.1 us (20%)
  between operations  0.71 us (2%)
    pallas_call x6, Pallas kernels, pinned(): run(*[pltpu.with_memory_space_constraint(v, pltpu.HBM) if spec is HB else...  17 us
    ppermute x5, starting transfers between devices, from_behind(): return lax.ppermute(value, axis, pairs)  8.05 us
    ppermute x5, waiting for transfers between devices, from_behind(): return lax.ppermute(value, axis, pairs)  7.1 us
    all_to_all x1, starting transfers between devices, on_device(): messages = lax.all_to_all(messages, ('dp', 'hst'), 0, 0, tiled=True)  2.7 us
  transfers between devices with their start and end apart: 6, of which 2 were waited for; matrix products, arithmetic and copies ran while one was open for 0% of the time, Pallas kernels for 46%

profile of v3, /device:TPU:0, one launch (start us, length us, event | category | flops | bytes accessed | tf_op | source)
XLA Modules:
  0.0 35.7 jit_solution(1188054445478338469)
XLA Ops:
  0.6 0.5 %collective-permute-start = (f32[256,1024]{1,0:T(8,128)}, f32[256,1024]{1,0:T(8,128)S(1)}, u32[]{:S(2)}, u32[]{:S(2)}) collective-permute-start(f32[256,1024]{1,0:T(8,128)} %bitcast.8), channel_id=1, source_target_pairs={{0,2},{2,4},{4,6},{6,8},{8,10},{10,12},{12,14},{14,16},{16,18},{18... | collective-permute-start | bytes 3145736 | tf_op jit(solution)/shard_map/ppermute | solution.py:18
  1.1 0.0 copy-start
  1.1 6.1 %shard_map.49 = (bf16[3,256,1024]{2,1,0:T(8,128)(2,1)S(1)}, f32[1,256]{1,0:T(1,128)S(1)}, f32[1,256]{1,0:T(1,128)S(1)}, f32[1,256]{1,0:T(1,128)S(1)}, f32[256,25...) custom-call(f32[256,1024]{1,0:T(8,128)} %bitcast.5, ...), custom_call_target="tpu_custom_call" | custom-call | flops 2415919104 | bytes 4194304 | tf_op jit(solution)/shard_map/pallas_call | solution.py:256
  7.2 2.7 %collective-permute-start.1 = (f32[1,256]{1,0:T(1,128)S(1)}, f32[1,256]{1,0:T(1,128)S(1)}, u32[]{:S(2)}, u32[]{:S(2)}) collective-permute-start(f32[1,256]{1,0:T(1,128)S(1)} %get-tuple-element.32.self_columns), channel_id=1, source_target_pairs={{0,2},{2,4},{4,6},{6,8},{8,10},{10,12},{12,14},{14,16},{16,18},{18... | collective-permute-start | bytes 3080 | tf_op jit(solution)/shard_map/ppermute | solution.py:18
  9.9 2.5 %collective-permute-start.2 = (f32[1,256]{1,0:T(1,128)S(1)}, f32[1,256]{1,0:T(1,128)S(1)}, u32[]{:S(2)}, u32[]{:S(2)}) collective-permute-start(f32[1,256]{1,0:T(1,128)S(1)} %get-tuple-element.33.self_rows), channel_id=1, source_target_pairs={{0,30},{2,0},{4,2},{6,4},{8,6},{10,8},{12,10},{14,12},{16,14},{18,... | collective-permute-start | bytes 3080 | tf_op jit(solution)/shard_map/ppermute | solution.py:18
  12.3 0.0 copy-done
  12.4 0.1 slice.8
  12.4 6.4 %collective-permute-done.1.before_columns = f32[1,256]{1,0:T(1,128)S(1)} collective-permute-done((f32[1,256]{1,0:T(1,128)S(1)}, f32[1,256]{1,0:T(1,128)S(1)}, u32[]{:S(2)}, u32[]{:S(2)}) %collective-permute-start.1) | collective-permute-done | bytes 1056 | tf_op jit(solution)/shard_map/ppermute | solution.py:18
  18.9 0.0 collective-permute-done.2.later_rows
  18.9 0.0 collective-permute-done.earlier_texts
  18.9 0.0 collective-permute-start.3
  18.9 2.4 %collective-permute-start.4 = (f32[256,256]{1,0:T(8,128)S(1)}, f32[256,256]{1,0:T(8,128)S(1)}, u32[]{:S(2)}, u32[]{:S(2)}) collective-permute-start(f32[256,256]{1,0:T(8,128)S(1)} %slice.9), channel_id=1, source_target_pairs={{0,30},{2,0},{4,2},{6,4},{8,6},{10,8},{12,10},{14,12},{16,14},{18,... | collective-permute-start | bytes 786440 | tf_op jit(solution)/shard_map/ppermute | solution.py:18
  21.3 2.0 %shard_map.50 = (f32[32,1,128]{2,1,0:T(1,128)}, f32[256,256]{1,0:T(8,128)S(1)}, f32[1,256]{1,0:T(1,128)S(1)}) custom-call(bf16[3,256,1024]{2,1,0:T(8,128)(2,1)S(1)} %get-tuple-element.35.image_parts, f32[256,1024]{1,0:T(8,128)S(1)} %collective-permute-done.earlier_texts, f32[1,256]{1,0:T(1,128)S(1)} %get-tuple-element.33.self_rows, ...), custom_call_target="tpu_custom_call" | custom-call | flops 805306368 | bytes 4194304 | tf_op jit(solution)/shard_map/pallas_call | solution.py:256
  23.3 2.7 %all-to-all-start = ((f32[32,1,128]{2,1,0:T(1,128)}), f32[32,1,128]{2,1,0:T(1,128)S(1)}, u32[]{:S(2)}, u32[]{:S(2)}) async-start(f32[32,1,128]{2,1,0:T(1,128)} %get-tuple-element.39), calls=%async_computation | async-start | bytes 32768 | tf_op jit(solution)/shard_map/all_to_all | solution.py:300
  26.0 3.5 %shard_map.51 = (f32[256,1024]{1,0:T(8,128)S(1)}, f32[256,1024]{1,0:T(8,128)S(1)}, bf16[3,256,1024]{2,1,0:T(8,128)(2,1)S(1)}, f32[256,256]{1,0:T(8,128)S(1)}) custom-call(f32[256,256]{1,0:T(8,128)S(1)} %get-tuple-element.40.weights, f32[256,1024]{1,0:T(8,128)S(1)} %collective-permute-done.earlier_texts, f32[1,256]{1,0:T(1,128)S(1)} %get-tuple-element.41.rows, ...), custom_call_target="tpu_custom_call" | custom-call | flops 1610612736 | bytes 4194304 | tf_op jit(solution)/shard_map/pallas_call | solution.py:256
  29.5 0.0 collective-permute-done.3.first
  29.5 1.2 %shard_map.52 = (bf16[3,256,1024]{2,1,0:T(8,128)(2,1)S(1)}, f32[256,256]{1,0:T(8,128)S(1)}, f32[256,1024]{1,0:T(8,128)S(1)}) custom-call(bf16[3,256,1024]{2,1,0:T(8,128)(2,1)S(1)} %get-tuple-element.46.text_parts, f32[256,768]{1,0:T(8,128)S(1)} %collective-permute-done.3.first, f32[256,1024]{1,0:T(8,128)} %get-tuple-element.48.column_store), custom_call_target="tpu_custom_call" | custom-call | flops 805306368 | bytes 4194304 | tf_op jit(solution)/shard_map/pallas_call | solution.py:256
  30.7 0.6 %collective-permute-done.4.second = f32[256,256]{1,0:T(8,128)S(1)} collective-permute-done((f32[256,256]{1,0:T(8,128)S(1)}, f32[256,256]{1,0:T(8,128)S(1)}, u32[]{:S(2)}, u32[]{:S(2)}) %collective-permute-start.4) | collective-permute-done | bytes 262176 | tf_op jit(solution)/shard_map/ppermute | solution.py:18
  31.4 3.8 %shard_map.53 = (bf16[3,256,1024]{2,1,0:T(8,128)(2,1)S(1)}, f32[256,1024]{1,0:T(8,128)}, f32[256,1024]{1,0:T(8,128)}) custom-call(bf16[3,256,1024]{2,1,0:T(8,128)(2,1)S(1)} %get-tuple-element.46.text_parts, bf16[3,256,1024]{2,1,0:T(8,128)(2,1)S(1)} %get-tuple-element.49.first_parts, ...), custom_call_target="tpu_custom_call", output_to_operand_aliasing={{0}: (1, {})} | custom-call | flops 2415919104 | bytes 4194304 | tf_op jit(solution)/shard_map/pallas_call | solution.py:256
  35.1 0.0 all-to-all-done.messages
  35.1 0.5 %shard_map.54 = f32[1,1]{1,0:T(1,128)} custom-call(f32[32,1,128]{2,1,0:T(1,128)S(1)} %all-to-all-done.messages), custom_call_target="tpu_custom_call" | custom-call | bytes 4194304 | tf_op jit(solution)/shard_map/pallas_call | solution.py:256
  (1 shorter events, 0.0 us)
Async XLA Ops:
  0.6 18.3 %collective-permute-start = (f32[256,1024]{1,0:T(8,128)}, f32[256,1024]{1,0:T(8,128)S(1)}, u32[]{:S(2)}, u32[]{:S(2)}) collective-permute-start(f32[256,1024]{1,0:T(8,128)} %bitcast.8), channel_id=1, source_target_pairs={{0,2},{2,4},{4,6},{6,8},{8,10},{10,12},{12,14},{14,16},{16,18},{18... | collective-permute-start | bytes 3145736 | tf_op jit(solution)/shard_map/ppermute | solution.py:18
  1.1 11.2 %copy-start = (f32[1,1,256,1024]{3,2,1,0:T(8,128)S(1)}, f32[1,1,256,1024]{3,2,1,0:T(8,128)}, u32[]{:S(2)}) copy-start(f32[1,1,256,1024]{3,2,1,0:T(8,128)} %param.2) | copy-start | bytes 3145732
  7.2 11.7 %collective-permute-start.1 = (f32[1,256]{1,0:T(1,128)S(1)}, f32[1,256]{1,0:T(1,128)S(1)}, u32[]{:S(2)}, u32[]{:S(2)}) collective-permute-start(f32[1,256]{1,0:T(1,128)S(1)} %get-tuple-element.32.self_columns), channel_id=1, source_target_pairs={{0,2},{2,4},{4,6},{6,8},{8,10},{10,12},{12,14},{14,16},{16,18},{18... | collective-permute-start | bytes 3080 | tf_op jit(solution)/shard_map/ppermute | solution.py:18
  9.9 9.0 %collective-permute-start.2 = (f32[1,256]{1,0:T(1,128)S(1)}, f32[1,256]{1,0:T(1,128)S(1)}, u32[]{:S(2)}, u32[]{:S(2)}) collective-permute-start(f32[1,256]{1,0:T(1,128)S(1)} %get-tuple-element.33.self_rows), channel_id=1, source_target_pairs={{0,30},{2,0},{4,2},{6,4},{8,6},{10,8},{12,10},{14,12},{16,14},{18,... | collective-permute-start | bytes 3080 | tf_op jit(solution)/shard_map/ppermute | solution.py:18
  18.9 10.6 %collective-permute-start.3 = (f32[256,768]{1,0:T(8,128)S(1)}, f32[256,768]{1,0:T(8,128)S(1)}, u32[]{:S(2)}, u32[]{:S(2)}) collective-permute-start(f32[256,768]{1,0:T(8,128)S(1)} %slice.8), channel_id=1, source_target_pairs={{0,30},{2,0},{4,2},{6,4},{8,6},{10,8},{12,10},{14,12},{16,14},{18,... | collective-permute-start | bytes 2359304 | tf_op jit(solution)/shard_map/ppermute | solution.py:18
  18.9 12.5 %collective-permute-start.4 = (f32[256,256]{1,0:T(8,128)S(1)}, f32[256,256]{1,0:T(8,128)S(1)}, u32[]{:S(2)}, u32[]{:S(2)}) collective-permute-start(f32[256,256]{1,0:T(8,128)S(1)} %slice.9), channel_id=1, source_target_pairs={{0,30},{2,0},{4,2},{6,4},{8,6},{10,8},{12,10},{14,12},{16,14},{18,... | collective-permute-start | bytes 786440 | tf_op jit(solution)/shard_map/ppermute | solution.py:18
  23.3 11.9 %all-to-all-start = ((f32[32,1,128]{2,1,0:T(1,128)}), f32[32,1,128]{2,1,0:T(1,128)S(1)}, u32[]{:S(2)}, u32[]{:S(2)}) async-start(f32[32,1,128]{2,1,0:T(1,128)} %get-tuple-element.39), calls=%async_computation | async-start | bytes 32768 | tf_op jit(solution)/shard_map/all_to_all | solution.py:300

commit v4 on v3

--- a/solution.py
+++ b/solution.py
@@ -62,6 +62,13 @@
     return largest + jnp.log(jnp.exp(former - largest) + jnp.exp(latter - largest))
 
 
+def joint_logsum(logits, other, axis):
+    largest = jnp.max(logits, axis=axis, keepdims=True)
+    powers = jnp.exp(logits - largest)
+    joint = paired_logsum(other, largest + jnp.log(jnp.sum(powers, axis=axis, keepdims=True)))
+    return joint, powers * (0.5 * jnp.exp(largest - joint))
+
+
 def diagonal_mask(count):
     shape = (count, count)
     return lax.broadcasted_iota(jnp.int32, shape, 0) == lax.broadcasted_iota(jnp.int32, shape, 1)
@@ -92,12 +99,15 @@
 
 def self_kernel(
     images, texts,
-    image_parts, row_part, positive, column_part, logits, image_store, text_store, row_product, column_term,
+    image_parts, row_part, columns_out, first, second, logits, image_store, text_store, row_product, column_term,
     own, image_in, text_in, text_parts, left, down, row_out, column_out, semaphores,
 ):
     copies = start([(images, image_in), (texts, text_in)], semaphores)
     copies[0].wait()
     store_parts(image_parts, image_in[...])
+    border = first.shape[1]
+    first[...] = image_in[:, :border]
+    sent = start([(image_in.at[:, border:], second)], semaphores.at[5:6])
     copies[1].wait()
     store_parts(text_parts, text_in[...])
     copies = start([(image_parts, image_store), (text_parts, text_store)], semaphores)
@@ -107,10 +117,10 @@
     rows, columns = logsum(block, 1), logsum(block, 0)
     own[...] = block
     row_part[...] = as_row(rows, diagonal)
-    column_part[...] = columns
-    positive[...] = as_row(block, diagonal)
-    left[...] = left_parts(0.5 * jnp.exp(block - rows))
-    down[...] = left_parts((0.5 * jnp.exp(block - columns)).T)
+    columns_out[0:1, :] = columns
+    columns_out[1:2, :] = as_row(block, diagonal)
+    left[...] = left_parts(jnp.where(diagonal, 0.0, 0.5 * jnp.exp(block - rows)))
+    down[...] = left_parts(jnp.where(diagonal, 0.0, 0.5 * jnp.exp(block - columns)).T)
     half = width // 2
 
     @pl.loop(0, 2)
@@ -120,19 +130,20 @@
         column_out[:, part] = rows_by_columns(down[...], image_parts.at[:, :, part])
 
     copies += start([(row_out, row_product), (column_out, column_term), (own, logits)], semaphores.at[2:5])
+    copies += sent
     for copy in copies:
         copy.wait()
 
 
 def earlier_kernel(
-    image_parts, earlier_texts, self_rows, before_columns, positive,
+    image_parts, earlier_texts, self_rows, self_columns, before_columns,
     messages, weights, rows_out,
 ):
     block = logit_scale * rows_by_rows(image_parts, split(earlier_texts[...]))
     diagonal = diagonal_mask(block.shape[0])
     rows = paired_logsum(self_rows[...], as_row(logsum(block, 1), diagonal))
-    columns = paired_logsum(before_columns[...], logsum(block, 0))
-    partial = jnp.sum(0.5 * (rows + columns) - positive[...], axis=1, keepdims=True)
+    columns = paired_logsum(before_columns[0:1, :], logsum(block, 0))
+    partial = 0.5 * jnp.sum((rows - self_columns[1:2, :]) + (columns - before_columns[1:2, :]), axis=1, keepdims=True)
     messages[...] = jnp.broadcast_to(partial, messages.shape)
     weights[...] = 0.5 * (jnp.exp(block - as_column(rows, diagonal)) + jnp.exp(block - columns))
     rows_out[...] = rows
@@ -160,7 +171,7 @@
         image_part[:, part] = rows_by_columns(left[...], earlier_parts.at[:, :, part])
 
     copies[0].wait()
-    down[...] = left_parts((0.5 * jnp.exp(own[...] - joint) - jnp.where(diagonal, 1.0, 0.0)).T)
+    down[...] = left_parts(jnp.where(diagonal, 0.0, 0.5 * jnp.exp(own[...] - joint)).T)
     copies[1].wait()
 
     @pl.loop(0, 2)
@@ -169,21 +180,21 @@
         row_term[:, part] = rows_by_columns(down[...], image_parts.at[:, :, part])
 
     copies[2].wait()
+    image_part[...] += scale * row_product[...]
     copies[3].wait()
-    whole = text_parts[0].astype(f32) + text_parts[1].astype(f32) + text_parts[2].astype(f32)
-    image_part[...] += scale * row_product[...] - whole
-
-
-def first_kernel(text_parts, first, column_store, later_parts, product, column_term, semaphores):
-    (copy,) = start([(column_store, column_term)], semaphores)
+
+
+def first_kernel(text_parts, first, column_store, images, later_parts, product, column_term, own_images, semaphores):
+    copies = start([(column_store, column_term), (images, own_images)], semaphores)
     part = slice(0, first.shape[1])
     store_parts(later_parts.at[:, :, part], first[...])
     product[...] = rows_by_rows(text_parts.at[:, :, part], later_parts.at[:, :, part])
-    copy.wait()
+    for copy in copies:
+        copy.wait()
 
 
 def last_kernel(
-    text_parts, first_parts, second, product, logits, later_rows, self_columns, image_part, row_term, column_term,
+    text_parts, first_parts, second, product, logits, rows_in, later_rows, self_columns, image_part, row_term, column_term, image_in,
     later_parts, image_grads, text_grads,
     left, own_left, image_out, text_out, semaphores,
 ):
@@ -192,11 +203,14 @@
     part = slice(width - second.shape[1], width)
     store_parts(later_parts.at[:, :, part], second[...])
     block = logit_scale * (product[...] + rows_by_rows(text_parts.at[:, :, part], later_parts.at[:, :, part]))
-    rows = paired_logsum(later_rows[...], logsum(block, 0))
-    own_columns = as_column(self_columns[...], diagonal)
-    columns = paired_logsum(own_columns, logsum(block, 1))
-    left[...] = left_parts(0.5 * (jnp.exp(block - rows) + jnp.exp(block - columns)))
-    own_left[...] = left_parts(0.5 * jnp.exp(logits[...] - as_row(columns, diagonal)))
+    own_columns = as_column(self_columns[0:1, :], diagonal)
+    rows, by_rows = joint_logsum(block, later_rows[...], 0)
+    columns, by_columns = joint_logsum(block, own_columns, 1)
+    left[...] = left_parts(by_rows + by_columns)
+    across, positive = as_row(columns, diagonal), self_columns[1:2, :]
+    own = 0.5 * (jnp.exp(positive - rows_in[...]) + jnp.exp(positive - across)) - 1.0
+    own_left[...] = left_parts(jnp.where(diagonal, own, 0.5 * jnp.exp(logits[...] - across)))
+    own_down = as_column(own, diagonal)
     scale = jnp.exp(own_columns - columns)
     half = width // 2
 
@@ -215,7 +229,8 @@
         image_out[:, part] = logit_scale * (image_part[:, part] + terms)
         of_image.start()
         terms = rows_by_columns(left[...], later_parts.at[:, :, part])
-        text_out[:, part] = logit_scale * (row_term[:, part] + scale * column_term[:, part] + terms)
+        own_terms = row_term[:, part] + scale * column_term[:, part] + own_down * image_in[:, part]
+        text_out[:, part] = logit_scale * (own_terms + terms)
         of_text.start()
 
     for k in range(2):
@@ -269,21 +284,20 @@
     devices = lax.axis_size("dp") * lax.axis_size("hst")
     earlier_texts = from_behind(texts, "dp", 1)
     (
-        image_parts, self_rows, positive, self_columns, logits, image_store, text_store, row_product, column_term
+        image_parts, self_rows, self_columns, first, second, logits, image_store, text_store, row_product, column_term
     ) = call(
         self_kernel,
         3,
         [HB, HB],
         [
-            (VM, *parts), (VM, *row), (VM, *row), (VM, *row),
-            (HB, *square), (HB, *parts), (HB, *parts), (HB, *whole), (HB, *whole),
+            (VM, *parts), (VM, *row), (VM, (2, count), f32),
+            (PV, (count, width - small), f32), (HB, (count, small), f32), (HB, *square), (HB, *parts), (HB, *parts), (HB, *whole), (HB, *whole),
         ],
         [square, whole, whole, parts, left, left, whole, whole],
-        5,
+        6,
     )(images, texts)
     before_columns = from_behind(self_columns, "dp", 1)
     later_rows = from_behind(self_rows, "dp", -1)
-    first, second = images[:, : width - small], images[:, width - small :]
     earlier_texts, first, second, before_columns, later_rows, image_parts = lax.optimization_barrier(
         (earlier_texts, first, second, before_columns, later_rows, image_parts)
     )
@@ -296,7 +310,7 @@
         [(PV, (devices, 1, LANES), f32), (VM, *square), (VM, *row)],
         [],
         0,
-    )(image_parts, earlier_texts, self_rows, before_columns, positive)
+    )(image_parts, earlier_texts, self_rows, self_columns, before_columns)
     messages = lax.all_to_all(messages, ("dp", "hst"), 0, 0, tiled=True)
     image_part, row_term, text_parts, logits = call(
         middle_kernel,
@@ -306,18 +320,20 @@
         [parts, parts, whole, left, left],
         4,
     )(weights, earlier_texts, rows, self_rows, logits, image_store, text_store, row_product)
-    later_parts, product, column_term = call(
-        first_kernel, 1, [VM, VM, HB], [(VM, *parts), (VM, *square), (VM, *whole)], [], 1
-    )(text_parts, first, column_term)
+    later_parts, product, column_term, images = call(
+        first_kernel, 1, [VM, VM, HB, HB], [(VM, *parts), (VM, *square), (VM, *whole), (VM, *whole)], [], 2
+    )(text_parts, first, column_term, images)
     _, image_grads, text_grads = call(
         last_kernel,
         3,
-        [VM] * 10,
+        [VM] * 12,
         [(VM, *parts), (HB, *whole), (HB, *whole)],
         [left, left, whole, whole],
         4,
         {1: 0},
-    )(text_parts, later_parts, second, product, logits, later_rows, self_columns, image_part, row_term, column_term)
+    )(
+        text_parts, later_parts, second, product, logits, rows, later_rows, self_columns, image_part, row_term, column_term, images
+    )
     messages, text_grads = lax.optimization_barrier((messages, text_grads))
     (mean_loss,) = call(functools.partial(loss_kernel, rows=count * devices), 0, [VM], [(VM, (1, 1), f32)], [], 0)(messages)
     return mean_loss[0, 0], image_grads[None, None], text_grads[None, None]

time: 35.9 us -> 36.1 us (level)
  transfers between devices with their start and end apart: 6 -> 6, of which waited for: 2 -> 3; matrix products, arithmetic and copies ran while one was open for 0% -> 0% of each run, Pallas kernels for 46% -> 47%
where the time goes in v4:
time: 36.1 us; the launch traced here: 35.9 us
  Pallas kernels  17.3 us (48%)
  starting transfers between devices  10.7 us (30%)
  waiting for transfers between devices  7.15 us (20%)
  between operations  0.69 us (2%)
    pallas_call x6, Pallas kernels, pinned(): run(*[pltpu.with_memory_space_constraint(v, pltpu.HBM) if spec is HB else...  17.3 us
    ppermute x5, starting transfers between devices, from_behind(): return lax.ppermute(value, axis, pairs)  8.05 us
    ppermute x5, waiting for transfers between devices, from_behind(): return lax.ppermute(value, axis, pairs)  7.15 us
    all_to_all x1, starting transfers between devices, on_device(): messages = lax.all_to_all(messages, ('dp', 'hst'), 0, 0, tiled=True)  2.68 us
  transfers between devices with their start and end apart: 6, of which 3 were waited for; matrix products, arithmetic and copies ran while one was open for 0% of the time, Pallas kernels for 47%

profile of v4, /device:TPU:0, one launch (start us, length us, event | category | flops | bytes accessed | tf_op | source)
XLA Modules:
  0.0 35.9 jit_solution(1317022104705957240)
XLA Ops:
  0.6 0.5 %collective-permute-start = (f32[256,1024]{1,0:T(8,128)}, f32[256,1024]{1,0:T(8,128)S(1)}, u32[]{:S(2)}, u32[]{:S(2)}) collective-permute-start(f32[256,1024]{1,0:T(8,128)} %bitcast.7), channel_id=1, source_target_pairs={{0,2},{2,4},{4,6},{6,8},{8,10},{10,12},{12,14},{14,16},{16,18},{18... | collective-permute-start | bytes 3145736 | tf_op jit(solution)/shard_map/ppermute | solution.py:18
  1.1 6.0 %shard_map.49 = (bf16[3,256,1024]{2,1,0:T(8,128)(2,1)S(1)}, f32[1,256]{1,0:T(1,128)S(1)}, f32[2,256]{1,0:T(2,128)S(1)}, f32[256,768]{1,0:T(8,128)S(1)}, f32[256,...) custom-call(f32[256,1024]{1,0:T(8,128)} %bitcast.5, ...), custom_call_target="tpu_custom_call" | custom-call | flops 2415919104 | bytes 4194304 | tf_op jit(solution)/shard_map/pallas_call | solution.py:271
  7.2 2.7 %collective-permute-start.1 = (f32[2,256]{1,0:T(2,128)S(1)}, f32[2,256]{1,0:T(2,128)S(1)}, u32[]{:S(2)}, u32[]{:S(2)}) collective-permute-start(f32[2,256]{1,0:T(2,128)S(1)} %get-tuple-element.36.self_columns), channel_id=1, source_target_pairs={{0,2},{2,4},{4,6},{6,8},{8,10},{10,12},{12,14},{14,16},{16,18},{18... | collective-permute-start | bytes 6152 | tf_op jit(solution)/shard_map/ppermute | solution.py:18
  9.8 2.5 %collective-permute-start.2 = (f32[1,256]{1,0:T(1,128)S(1)}, f32[1,256]{1,0:T(1,128)S(1)}, u32[]{:S(2)}, u32[]{:S(2)}) collective-permute-start(f32[1,256]{1,0:T(1,128)S(1)} %get-tuple-element.37.self_rows), channel_id=1, source_target_pairs={{0,30},{2,0},{4,2},{6,4},{8,6},{10,8},{12,10},{14,12},{16,14},{18,... | collective-permute-start | bytes 3080 | tf_op jit(solution)/shard_map/ppermute | solution.py:18
  12.3 1.3 %collective-permute-done.2.later_rows = f32[1,256]{1,0:T(1,128)S(1)} collective-permute-done((f32[1,256]{1,0:T(1,128)S(1)}, f32[1,256]{1,0:T(1,128)S(1)}, u32[]{:S(2)}, u32[]{:S(2)}) %collective-permute-start.2) | collective-permute-done | bytes 1056 | tf_op jit(solution)/shard_map/ppermute | solution.py:18
  13.6 5.3 %collective-permute-done.1.before_columns = f32[2,256]{1,0:T(2,128)S(1)} collective-permute-done((f32[2,256]{1,0:T(2,128)S(1)}, f32[2,256]{1,0:T(2,128)S(1)}, u32[]{:S(2)}, u32[]{:S(2)}) %collective-permute-start.1) | collective-permute-done | bytes 2080 | tf_op jit(solution)/shard_map/ppermute | solution.py:18
  18.9 0.0 collective-permute-done.earlier_texts
  18.9 0.0 collective-permute-start.3
  18.9 2.4 %collective-permute-start.4 = (f32[256,256]{1,0:T(8,128)}, f32[256,256]{1,0:T(8,128)S(1)}, u32[]{:S(2)}, u32[]{:S(2)}) collective-permute-start(f32[256,256]{1,0:T(8,128)} %get-tuple-element.53), channel_id=1, source_target_pairs={{0,30},{2,0},{4,2},{6,4},{8,6},{10,8},{12,10},{14,12},{16,14},{18,... | collective-permute-start | bytes 786440 | tf_op jit(solution)/shard_map/ppermute | solution.py:18
  21.3 2.0 %shard_map.50 = (f32[32,1,128]{2,1,0:T(1,128)}, f32[256,256]{1,0:T(8,128)S(1)}, f32[1,256]{1,0:T(1,128)S(1)}) custom-call(bf16[3,256,1024]{2,1,0:T(8,128)(2,1)S(1)} %get-tuple-element.39.image_parts, f32[256,1024]{1,0:T(8,128)S(1)} %collective-permute-done.earlier_texts, f32[1,256]{1,0:T(1,128)S(1)} %get-tuple-element.37.self_rows, ...), custom_call_target="tpu_custom_call" | custom-call | flops 805306368 | bytes 4194304 | tf_op jit(solution)/shard_map/pallas_call | solution.py:271
  23.3 2.7 %all-to-all-start = ((f32[32,1,128]{2,1,0:T(1,128)}), f32[32,1,128]{2,1,0:T(1,128)S(1)}, u32[]{:S(2)}, u32[]{:S(2)}) async-start(f32[32,1,128]{2,1,0:T(1,128)} %get-tuple-element.42), calls=%async_computation | async-start | bytes 32768 | tf_op jit(solution)/shard_map/all_to_all | solution.py:314
  25.9 3.3 %shard_map.51 = (f32[256,1024]{1,0:T(8,128)S(1)}, f32[256,1024]{1,0:T(8,128)S(1)}, bf16[3,256,1024]{2,1,0:T(8,128)(2,1)S(1)}, f32[256,256]{1,0:T(8,128)S(1)}) custom-call(f32[256,256]{1,0:T(8,128)S(1)} %get-tuple-element.43.weights, f32[256,1024]{1,0:T(8,128)S(1)} %collective-permute-done.earlier_texts, f32[1,256]{1,0:T(1,128)S(1)} %get-tuple-element.44.rows.rows_in, ...), custom_call_target="tpu_custom_call" | custom-call | flops 1610612736 | bytes 4194304 | tf_op jit(solution)/shard_map/pallas_call | solution.py:271
  29.3 0.0 collective-permute-done.3.first
  29.3 1.6 %shard_map.52 = (bf16[3,256,1024]{2,1,0:T(8,128)(2,1)S(1)}, f32[256,256]{1,0:T(8,128)S(1)}, f32[256,1024]{1,0:T(8,128)S(1)}, f32[256,1024]{1,0:T(8,128)S(1)}) custom-call(bf16[3,256,1024]{2,1,0:T(8,128)(2,1)S(1)} %get-tuple-element.49.text_parts, f32[256,768]{1,0:T(8,128)S(1)} %collective-permute-done.3.first, f32[256,1024]{1,0:T(8,128)} %get-tuple-element.51.column_store, ...), custom_call_target="tpu_custom_call" | custom-call | flops 805306368 | bytes 4194304 | tf_op jit(solution)/shard_map/pallas_call | solution.py:271
  30.9 0.6 %collective-permute-done.4.second = f32[256,256]{1,0:T(8,128)S(1)} collective-permute-done((f32[256,256]{1,0:T(8,128)}, f32[256,256]{1,0:T(8,128)S(1)}, u32[]{:S(2)}, u32[]{:S(2)}) %collective-permute-start.4) | collective-permute-done | bytes 262176 | tf_op jit(solution)/shard_map/ppermute | solution.py:18
  31.4 3.9 %shard_map.53 = (bf16[3,256,1024]{2,1,0:T(8,128)(2,1)S(1)}, f32[256,1024]{1,0:T(8,128)}, f32[256,1024]{1,0:T(8,128)}) custom-call(bf16[3,256,1024]{2,1,0:T(8,128)(2,1)S(1)} %get-tuple-element.49.text_parts, bf16[3,256,1024]{2,1,0:T(8,128)(2,1)S(1)} %get-tuple-element.52.first_parts, ...), custom_call_target="tpu_custom_call", output_to_operand_aliasing={{0}: (1, {})} | custom-call | flops 2415919104 | bytes 4194304 | tf_op jit(solution)/shard_map/pallas_call | solution.py:271
  35.3 0.0 all-to-all-done.messages
  35.3 0.5 %shard_map.54 = f32[1,1]{1,0:T(1,128)} custom-call(f32[32,1,128]{2,1,0:T(1,128)S(1)} %all-to-all-done.messages), custom_call_target="tpu_custom_call" | custom-call | bytes 4194304 | tf_op jit(solution)/shard_map/pallas_call | solution.py:271
Async XLA Ops:
  0.6 18.2 %collective-permute-start = (f32[256,1024]{1,0:T(8,128)}, f32[256,1024]{1,0:T(8,128)S(1)}, u32[]{:S(2)}, u32[]{:S(2)}) collective-permute-start(f32[256,1024]{1,0:T(8,128)} %bitcast.7), channel_id=1, source_target_pairs={{0,2},{2,4},{4,6},{6,8},{8,10},{10,12},{12,14},{14,16},{16,18},{18... | collective-permute-start | bytes 3145736 | tf_op jit(solution)/shard_map/ppermute | solution.py:18
  7.2 11.7 %collective-permute-start.1 = (f32[2,256]{1,0:T(2,128)S(1)}, f32[2,256]{1,0:T(2,128)S(1)}, u32[]{:S(2)}, u32[]{:S(2)}) collective-permute-start(f32[2,256]{1,0:T(2,128)S(1)} %get-tuple-element.36.self_columns), channel_id=1, source_target_pairs={{0,2},{2,4},{4,6},{6,8},{8,10},{10,12},{12,14},{14,16},{16,18},{18... | collective-permute-start | bytes 6152 | tf_op jit(solution)/shard_map/ppermute | solution.py:18
  9.8 3.8 %collective-permute-start.2 = (f32[1,256]{1,0:T(1,128)S(1)}, f32[1,256]{1,0:T(1,128)S(1)}, u32[]{:S(2)}, u32[]{:S(2)}) collective-permute-start(f32[1,256]{1,0:T(1,128)S(1)} %get-tuple-element.37.self_rows), channel_id=1, source_target_pairs={{0,30},{2,0},{4,2},{6,4},{8,6},{10,8},{12,10},{14,12},{16,14},{18,... | collective-permute-start | bytes 3080 | tf_op jit(solution)/shard_map/ppermute | solution.py:18
  18.9 10.4 %collective-permute-start.3 = (f32[256,768]{1,0:T(8,128)S(1)}, f32[256,768]{1,0:T(8,128)S(1)}, u32[]{:S(2)}, u32[]{:S(2)}) collective-permute-start(f32[256,768]{1,0:T(8,128)S(1)} %get-tuple-element.50), channel_id=1, source_target_pairs={{0,30},{2,0},{4,2},{6,4},{8,6},{10,8},{12,10},{14,12},{16,14},{18,... | collective-permute-start | bytes 2359304 | tf_op jit(solution)/shard_map/ppermute | solution.py:18
  18.9 12.6 %collective-permute-start.4 = (f32[256,256]{1,0:T(8,128)}, f32[256,256]{1,0:T(8,128)S(1)}, u32[]{:S(2)}, u32[]{:S(2)}) collective-permute-start(f32[256,256]{1,0:T(8,128)} %get-tuple-element.53), channel_id=1, source_target_pairs={{0,30},{2,0},{4,2},{6,4},{8,6},{10,8},{12,10},{14,12},{16,14},{18,... | collective-permute-start | bytes 786440 | tf_op jit(solution)/shard_map/ppermute | solution.py:18
  23.3 12.1 %all-to-all-start = ((f32[32,1,128]{2,1,0:T(1,128)}), f32[32,1,128]{2,1,0:T(1,128)S(1)}, u32[]{:S(2)}, u32[]{:S(2)}) async-start(f32[32,1,128]{2,1,0:T(1,128)} %get-tuple-element.42), calls=%async_computation | async-start | bytes 32768 | tf_op jit(solution)/shard_map/all_to_all | solution.py:314

commit v5 on v4

--- a/solution.py
+++ b/solution.py
@@ -107,7 +107,7 @@
     store_parts(image_parts, image_in[...])
     border = first.shape[1]
     first[...] = image_in[:, :border]
-    sent = start([(image_in.at[:, border:], second)], semaphores.at[5:6])
+    second[...] = image_in[:, border:]
     copies[1].wait()
     store_parts(text_parts, text_in[...])
     copies = start([(image_parts, image_store), (text_parts, text_store)], semaphores)
@@ -130,7 +130,6 @@
         column_out[:, part] = rows_by_columns(down[...], image_parts.at[:, :, part])
 
     copies += start([(row_out, row_product), (column_out, column_term), (own, logits)], semaphores.at[2:5])
-    copies += sent
     for copy in copies:
         copy.wait()
 
@@ -138,15 +137,18 @@
 def earlier_kernel(
     image_parts, earlier_texts, self_rows, self_columns, before_columns,
     messages, weights, rows_out,
+    letters, semaphores,
 ):
     block = logit_scale * rows_by_rows(image_parts, split(earlier_texts[...]))
     diagonal = diagonal_mask(block.shape[0])
     rows = paired_logsum(self_rows[...], as_row(logsum(block, 1), diagonal))
     columns = paired_logsum(before_columns[0:1, :], logsum(block, 0))
     partial = 0.5 * jnp.sum((rows - self_columns[1:2, :]) + (columns - before_columns[1:2, :]), axis=1, keepdims=True)
-    messages[...] = jnp.broadcast_to(partial, messages.shape)
+    letters[...] = jnp.broadcast_to(partial, letters.shape)
+    (copy,) = start([(letters, messages)], semaphores)
     weights[...] = 0.5 * (jnp.exp(block - as_column(rows, diagonal)) + jnp.exp(block - columns))
     rows_out[...] = rows
+    copy.wait()
 
 
 def middle_kernel(
@@ -291,7 +293,7 @@
         [HB, HB],
         [
             (VM, *parts), (VM, *row), (VM, (2, count), f32),
-            (PV, (count, width - small), f32), (HB, (count, small), f32), (HB, *square), (HB, *parts), (HB, *parts), (HB, *whole), (HB, *whole),
+            (PV, (count, width - small), f32), (PV, (count, small), f32), (HB, *square), (HB, *parts), (HB, *parts), (HB, *whole), (HB, *whole),
         ],
         [square, whole, whole, parts, left, left, whole, whole],
         6,
@@ -302,15 +304,16 @@
         (earlier_texts, first, second, before_columns, later_rows, image_parts)
     )
     first = from_behind(first, "dp", -1)
-    second = from_behind(second, "dp", -1)
     messages, weights, rows = call(
         earlier_kernel,
         1,
         [VM] * 5,
-        [(PV, (devices, 1, LANES), f32), (VM, *square), (VM, *row)],
-        [],
-        0,
+        [(HB, (devices, 1, LANES), f32), (VM, *square), (VM, *row)],
+        [((devices, 1, LANES), f32)],
+        1,
     )(image_parts, earlier_texts, self_rows, self_columns, before_columns)
+    second, weights = lax.optimization_barrier((second, weights))
+    second = from_behind(second, "dp", -1)
     messages = lax.all_to_all(messages, ("dp", "hst"), 0, 0, tiled=True)
     image_part, row_term, text_parts, logits = call(
         middle_kernel,

time: 36.1 us -> 35.9 us (level)
  no operation moved by 1% of the time
where the time goes in v5:
time: 35.9 us; the launch traced here: 35.7 us
  Pallas kernels  17.4 us (48%)
  starting transfers between devices  10.8 us (30%)
  waiting for transfers between devices  6.85 us (19%)
  between operations  0.7 us (2%)
    pallas_call x6, Pallas kernels, pinned(): run(*[pltpu.with_memory_space_constraint(v, pltpu.HBM) if spec is HB else...  17.4 us
    ppermute x5, starting transfers between devices, from_behind(): return lax.ppermute(value, axis, pairs)  8.1 us
    ppermute x5, waiting for transfers between devices, from_behind(): return lax.ppermute(value, axis, pairs)  6.85 us
    all_to_all x1, starting transfers between devices, on_device(): messages = lax.all_to_all(messages, ('dp', 'hst'), 0, 0, tiled=True)  2.69 us
  transfers between devices with their start and end apart: 6, of which 3 were waited for; matrix products, arithmetic and copies ran while one was open for 0% of the time, Pallas kernels for 47%

profile of v5, /device:TPU:0, one launch (start us, length us, event | category | flops | bytes accessed | tf_op | source)
XLA Modules:
  0.0 35.7 jit_solution(14028644324011874347)
XLA Ops:
  0.6 0.5 %collective-permute-start = (f32[256,1024]{1,0:T(8,128)}, f32[256,1024]{1,0:T(8,128)S(1)}, u32[]{:S(2)}, u32[]{:S(2)}) collective-permute-start(f32[256,1024]{1,0:T(8,128)} %bitcast.7), channel_id=1, source_target_pairs={{0,2},{2,4},{4,6},{6,8},{8,10},{10,12},{12,14},{14,16},{16,18},{18... | collective-permute-start | bytes 3145736 | tf_op jit(solution)/shard_map/ppermute | solution.py:18
  1.1 6.1 %shard_map.49 = (bf16[3,256,1024]{2,1,0:T(8,128)(2,1)S(1)}, f32[1,256]{1,0:T(1,128)S(1)}, f32[2,256]{1,0:T(2,128)S(1)}, f32[256,768]{1,0:T(8,128)S(1)}, f32[256,...) custom-call(f32[256,1024]{1,0:T(8,128)} %bitcast.5, ...), custom_call_target="tpu_custom_call" | custom-call | flops 2415919104 | bytes 4194304 | tf_op jit(solution)/shard_map/pallas_call | solution.py:273
  7.2 2.7 %collective-permute-start.1 = (f32[2,256]{1,0:T(2,128)S(1)}, f32[2,256]{1,0:T(2,128)S(1)}, u32[]{:S(2)}, u32[]{:S(2)}) collective-permute-start(f32[2,256]{1,0:T(2,128)S(1)} %get-tuple-element.38.self_columns), channel_id=1, source_target_pairs={{0,2},{2,4},{4,6},{6,8},{8,10},{10,12},{12,14},{14,16},{16,18},{18... | collective-permute-start | bytes 6152 | tf_op jit(solution)/shard_map/ppermute | solution.py:18
  9.9 2.4 %collective-permute-start.2 = (f32[1,256]{1,0:T(1,128)S(1)}, f32[1,256]{1,0:T(1,128)S(1)}, u32[]{:S(2)}, u32[]{:S(2)}) collective-permute-start(f32[1,256]{1,0:T(1,128)S(1)} %get-tuple-element.39.self_rows), channel_id=1, source_target_pairs={{0,30},{2,0},{4,2},{6,4},{8,6},{10,8},{12,10},{14,12},{16,14},{18,... | collective-permute-start | bytes 3080 | tf_op jit(solution)/shard_map/ppermute | solution.py:18
  12.3 1.3 %collective-permute-done.2.later_rows = f32[1,256]{1,0:T(1,128)S(1)} collective-permute-done((f32[1,256]{1,0:T(1,128)S(1)}, f32[1,256]{1,0:T(1,128)S(1)}, u32[]{:S(2)}, u32[]{:S(2)}) %collective-permute-start.2) | collective-permute-done | bytes 1056 | tf_op jit(solution)/shard_map/ppermute | solution.py:18
  13.6 5.2 %collective-permute-done.1.before_columns = f32[2,256]{1,0:T(2,128)S(1)} collective-permute-done((f32[2,256]{1,0:T(2,128)S(1)}, f32[2,256]{1,0:T(2,128)S(1)}, u32[]{:S(2)}, u32[]{:S(2)}) %collective-permute-start.1) | collective-permute-done | bytes 2080 | tf_op jit(solution)/shard_map/ppermute | solution.py:18
  18.9 0.0 collective-permute-done.earlier_texts
  18.9 0.0 collective-permute-start.3
  18.9 2.0 %shard_map.50 = (f32[32,1,128]{2,1,0:T(1,128)}, f32[256,256]{1,0:T(8,128)S(1)}, f32[1,256]{1,0:T(1,128)S(1)}) custom-call(bf16[3,256,1024]{2,1,0:T(8,128)(2,1)S(1)} %get-tuple-element.41.image_parts, f32[256,1024]{1,0:T(8,128)S(1)} %collective-permute-done.earlier_texts, f32[1,256]{1,0:T(1,128)S(1)} %get-tuple-element.39.self_rows, ...), custom_call_target="tpu_custom_call" | custom-call | flops 805306368 | bytes 4194304 | tf_op jit(solution)/shard_map/pallas_call | solution.py:273
  20.9 2.5 %collective-permute-start.4 = (f32[256,256]{1,0:T(8,128)S(1)}, f32[256,256]{1,0:T(8,128)S(1)}, u32[]{:S(2)}, u32[]{:S(2)}) collective-permute-start(f32[256,256]{1,0:T(8,128)S(1)} %get-tuple-element.57), channel_id=1, source_target_pairs={{0,30},{2,0},{4,2},{6,4},{8,6},{10,8},{12,10},{14,12},{16,14},{18,... | collective-permute-start | bytes 786440 | tf_op jit(solution)/shard_map/ppermute | solution.py:18
  23.4 2.7 %all-to-all-start = ((f32[32,1,128]{2,1,0:T(1,128)}), f32[32,1,128]{2,1,0:T(1,128)S(1)}, u32[]{:S(2)}, u32[]{:S(2)}) async-start(f32[32,1,128]{2,1,0:T(1,128)} %get-tuple-element.44), calls=%async_computation | async-start | bytes 32768 | tf_op jit(solution)/shard_map/all_to_all | solution.py:317
  26.1 3.4 %shard_map.51 = (f32[256,1024]{1,0:T(8,128)S(1)}, f32[256,1024]{1,0:T(8,128)S(1)}, bf16[3,256,1024]{2,1,0:T(8,128)(2,1)S(1)}, f32[256,256]{1,0:T(8,128)S(1)}) custom-call(f32[256,256]{1,0:T(8,128)S(1)} %get-tuple-element.47.weights, f32[256,1024]{1,0:T(8,128)S(1)} %collective-permute-done.earlier_texts, f32[1,256]{1,0:T(1,128)S(1)} %get-tuple-element.48.rows.rows_in, ...), custom_call_target="tpu_custom_call" | custom-call | flops 1610612736 | bytes 4194304 | tf_op jit(solution)/shard_map/pallas_call | solution.py:273
  29.4 0.0 collective-permute-done.3.first
  29.4 1.6 %shard_map.52 = (bf16[3,256,1024]{2,1,0:T(8,128)(2,1)S(1)}, f32[256,256]{1,0:T(8,128)S(1)}, f32[256,1024]{1,0:T(8,128)S(1)}, f32[256,1024]{1,0:T(8,128)S(1)}) custom-call(bf16[3,256,1024]{2,1,0:T(8,128)(2,1)S(1)} %get-tuple-element.53.text_parts, f32[256,768]{1,0:T(8,128)S(1)} %collective-permute-done.3.first, f32[256,1024]{1,0:T(8,128)} %get-tuple-element.55.column_store, ...), custom_call_target="tpu_custom_call" | custom-call | flops 805306368 | bytes 4194304 | tf_op jit(solution)/shard_map/pallas_call | solution.py:273
  31.0 0.3 collective-permute-done.4.second
  31.3 3.8 %shard_map.53 = (bf16[3,256,1024]{2,1,0:T(8,128)(2,1)S(1)}, f32[256,1024]{1,0:T(8,128)}, f32[256,1024]{1,0:T(8,128)}) custom-call(bf16[3,256,1024]{2,1,0:T(8,128)(2,1)S(1)} %get-tuple-element.53.text_parts, bf16[3,256,1024]{2,1,0:T(8,128)(2,1)S(1)} %get-tuple-element.56.first_parts, ...), custom_call_target="tpu_custom_call", output_to_operand_aliasing={{0}: (1, {})} | custom-call | flops 2415919104 | bytes 4194304 | tf_op jit(solution)/shard_map/pallas_call | solution.py:273
  35.2 0.0 all-to-all-done.messages
  35.2 0.5 %shard_map.54 = f32[1,1]{1,0:T(1,128)} custom-call(f32[32,1,128]{2,1,0:T(1,128)S(1)} %all-to-all-done.messages), custom_call_target="tpu_custom_call" | custom-call | bytes 4194304 | tf_op jit(solution)/shard_map/pallas_call | solution.py:273
Async XLA Ops:
  0.6 18.2 %collective-permute-start = (f32[256,1024]{1,0:T(8,128)}, f32[256,1024]{1,0:T(8,128)S(1)}, u32[]{:S(2)}, u32[]{:S(2)}) collective-permute-start(f32[256,1024]{1,0:T(8,128)} %bitcast.7), channel_id=1, source_target_pairs={{0,2},{2,4},{4,6},{6,8},{8,10},{10,12},{12,14},{14,16},{16,18},{18... | collective-permute-start | bytes 3145736 | tf_op jit(solution)/shard_map/ppermute | solution.py:18
  7.2 11.6 %collective-permute-start.1 = (f32[2,256]{1,0:T(2,128)S(1)}, f32[2,256]{1,0:T(2,128)S(1)}, u32[]{:S(2)}, u32[]{:S(2)}) collective-permute-start(f32[2,256]{1,0:T(2,128)S(1)} %get-tuple-element.38.self_columns), channel_id=1, source_target_pairs={{0,2},{2,4},{4,6},{6,8},{8,10},{10,12},{12,14},{14,16},{16,18},{18... | collective-permute-start | bytes 6152 | tf_op jit(solution)/shard_map/ppermute | solution.py:18
  9.9 3.7 %collective-permute-start.2 = (f32[1,256]{1,0:T(1,128)S(1)}, f32[1,256]{1,0:T(1,128)S(1)}, u32[]{:S(2)}, u32[]{:S(2)}) collective-permute-start(f32[1,256]{1,0:T(1,128)S(1)} %get-tuple-element.39.self_rows), channel_id=1, source_target_pairs={{0,30},{2,0},{4,2},{6,4},{8,6},{10,8},{12,10},{14,12},{16,14},{18,... | collective-permute-start | bytes 3080 | tf_op jit(solution)/shard_map/ppermute | solution.py:18
  18.9 10.6 %collective-permute-start.3 = (f32[256,768]{1,0:T(8,128)S(1)}, f32[256,768]{1,0:T(8,128)S(1)}, u32[]{:S(2)}, u32[]{:S(2)}) collective-permute-start(f32[256,768]{1,0:T(8,128)S(1)} %get-tuple-element.54), channel_id=1, source_target_pairs={{0,30},{2,0},{4,2},{6,4},{8,6},{10,8},{12,10},{14,12},{16,14},{18,... | collective-permute-start | bytes 2359304 | tf_op jit(solution)/shard_map/ppermute | solution.py:18
  20.9 10.4 %collective-permute-start.4 = (f32[256,256]{1,0:T(8,128)S(1)}, f32[256,256]{1,0:T(8,128)S(1)}, u32[]{:S(2)}, u32[]{:S(2)}) collective-permute-start(f32[256,256]{1,0:T(8,128)S(1)} %get-tuple-element.57), channel_id=1, source_target_pairs={{0,30},{2,0},{4,2},{6,4},{8,6},{10,8},{12,10},{14,12},{16,14},{18,... | collective-permute-start | bytes 786440 | tf_op jit(solution)/shard_map/ppermute | solution.py:18
  23.4 11.8 %all-to-all-start = ((f32[32,1,128]{2,1,0:T(1,128)}), f32[32,1,128]{2,1,0:T(1,128)S(1)}, u32[]{:S(2)}, u32[]{:S(2)}) async-start(f32[32,1,128]{2,1,0:T(1,128)} %get-tuple-element.44), calls=%async_computation | async-start | bytes 32768 | tf_op jit(solution)/shard_map/all_to_all | solution.py:317

commit v6 on v5

--- a/solution.py
+++ b/solution.py
@@ -186,23 +186,24 @@
     copies[3].wait()
 
 
-def first_kernel(text_parts, first, column_store, images, later_parts, product, column_term, own_images, semaphores):
+def first_kernel(text_parts, first, column_store, images, first_parts, product, column_term, own_images, semaphores):
     copies = start([(column_store, column_term), (images, own_images)], semaphores)
-    part = slice(0, first.shape[1])
-    store_parts(later_parts.at[:, :, part], first[...])
-    product[...] = rows_by_rows(text_parts.at[:, :, part], later_parts.at[:, :, part])
+    store_parts(first_parts, first[...])
+    product[...] = rows_by_rows(text_parts.at[:, :, : first.shape[1]], first_parts)
     for copy in copies:
         copy.wait()
 
 
 def last_kernel(
     text_parts, first_parts, second, product, logits, rows_in, later_rows, self_columns, image_part, row_term, column_term, image_in,
-    later_parts, image_grads, text_grads,
-    left, own_left, image_out, text_out, semaphores,
+    image_grads, text_grads,
+    later_parts, left, own_left, image_out, text_out, semaphores,
 ):
     count, width = image_out.shape
     diagonal = diagonal_mask(count)
-    part = slice(width - second.shape[1], width)
+    border = first_parts.shape[2]
+    part = slice(border, width)
+    later_parts[:, :, :border] = first_parts[...]
     store_parts(later_parts.at[:, :, part], second[...])
     block = logit_scale * (product[...] + rows_by_rows(text_parts.at[:, :, part], later_parts.at[:, :, part]))
     own_columns = as_column(self_columns[0:1, :], diagonal)
@@ -247,7 +248,7 @@
 VM, PV, HB = (pl.BlockSpec(memory_space=place) for place in (pltpu.VMEM, pltpu.VMEM, pltpu.HBM))
 
 
-def call(kernel, products, ins, outs, scratch, copies, aliases=None):
+def call(kernel, products, ins, outs, scratch, copies):
     def shape_of(place, shape, dtype):
         if place is HB:
             return pltpu.HBM(shape, dtype)
@@ -259,7 +260,6 @@
         kernel,
         out_shape=[shape_of(*out) for out in outs],
         in_specs=ins,
-        input_output_aliases=aliases or {},
         out_specs=[out[0] for out in outs],
         scratch_shapes=[pltpu.VMEM(shape, dtype) for shape, dtype in scratch]
         + ([pltpu.SemaphoreType.DMA((copies,))] if copies else []),
@@ -323,19 +323,23 @@
         [parts, parts, whole, left, left],
         4,
     )(weights, earlier_texts, rows, self_rows, logits, image_store, text_store, row_product)
-    later_parts, product, column_term, images = call(
-        first_kernel, 1, [VM, VM, HB, HB], [(VM, *parts), (VM, *square), (VM, *whole), (VM, *whole)], [], 2
+    first_parts, product, column_term, images = call(
+        first_kernel,
+        1,
+        [VM, VM, HB, HB],
+        [(VM, (3, count, width - small), bf16), (VM, *square), (VM, *whole), (VM, *whole)],
+        [],
+        2,
     )(text_parts, first, column_term, images)
-    _, image_grads, text_grads = call(
+    image_grads, text_grads = call(
         last_kernel,
         3,
         [VM] * 12,
-        [(VM, *parts), (HB, *whole), (HB, *whole)],
-        [left, left, whole, whole],
+        [(HB, *whole), (HB, *whole)],
+        [parts, left, left, whole, whole],
         4,
-        {1: 0},
     )(
-        text_parts, later_parts, second, product, logits, rows, later_rows, self_columns, image_part, row_term, column_term, images
+        text_parts, first_parts, second, product, logits, rows, later_rows, self_columns, image_part, row_term, column_term, images
     )
     messages, text_grads = lax.optimization_barrier((messages, text_grads))
     (mean_loss,) = call(functools.partial(loss_kernel, rows=count * devices), 0, [VM], [(VM, (1, 1), f32)], [], 0)(messages)

time: 35.9 us -> 36 us (level)
  no operation moved by 1% of the time
where the time goes in v6:
time: 36 us; the launch traced here: 35.8 us
  Pallas kernels  17.5 us (49%)
  starting transfers between devices  10.8 us (30%)
  waiting for transfers between devices  6.85 us (19%)
  between operations  0.7 us (2%)
    pallas_call x6, Pallas kernels, pinned(): run(*[pltpu.with_memory_space_constraint(v, pltpu.HBM) if spec is HB else...  17.5 us
    ppermute x5, starting transfers between devices, from_behind(): return lax.ppermute(value, axis, pairs)  8.1 us
    ppermute x5, waiting for transfers between devices, from_behind(): return lax.ppermute(value, axis, pairs)  6.85 us
    all_to_all x1, starting transfers between devices, on_device(): messages = lax.all_to_all(messages, ('dp', 'hst'), 0, 0, tiled=True)  2.69 us
  transfers between devices with their start and end apart: 6, of which 3 were waited for; matrix products, arithmetic and copies ran while one was open for 0% of the time, Pallas kernels for 47%

profile of v6, /device:TPU:0, one launch (start us, length us, event | category | flops | bytes accessed | tf_op | source)
XLA Modules:
  0.0 35.8 jit_solution(2223767389466098594)
XLA Ops:
  0.6 0.5 %collective-permute-start = (f32[256,1024]{1,0:T(8,128)}, f32[256,1024]{1,0:T(8,128)S(1)}, u32[]{:S(2)}, u32[]{:S(2)}) collective-permute-start(f32[256,1024]{1,0:T(8,128)} %bitcast.7), channel_id=1, source_target_pairs={{0,2},{2,4},{4,6},{6,8},{8,10},{10,12},{12,14},{14,16},{16,18},{18... | collective-permute-start | bytes 3145736 | tf_op jit(solution)/shard_map/ppermute | solution.py:18
  1.1 6.1 %shard_map.49 = (bf16[3,256,1024]{2,1,0:T(8,128)(2,1)S(1)}, f32[1,256]{1,0:T(1,128)S(1)}, f32[2,256]{1,0:T(2,128)S(1)}, f32[256,768]{1,0:T(8,128)S(1)}, f32[256,...) custom-call(f32[256,1024]{1,0:T(8,128)} %bitcast.5, ...), custom_call_target="tpu_custom_call" | custom-call | flops 2415919104 | bytes 4194304 | tf_op jit(solution)/shard_map/pallas_call | solution.py:273
  7.2 2.7 %collective-permute-start.1 = (f32[2,256]{1,0:T(2,128)S(1)}, f32[2,256]{1,0:T(2,128)S(1)}, u32[]{:S(2)}, u32[]{:S(2)}) collective-permute-start(f32[2,256]{1,0:T(2,128)S(1)} %get-tuple-element.38.self_columns), channel_id=1, source_target_pairs={{0,2},{2,4},{4,6},{6,8},{8,10},{10,12},{12,14},{14,16},{16,18},{18... | collective-permute-start | bytes 6152 | tf_op jit(solution)/shard_map/ppermute | solution.py:18
  9.9 2.4 %collective-permute-start.2 = (f32[1,256]{1,0:T(1,128)S(1)}, f32[1,256]{1,0:T(1,128)S(1)}, u32[]{:S(2)}, u32[]{:S(2)}) collective-permute-start(f32[1,256]{1,0:T(1,128)S(1)} %get-tuple-element.39.self_rows), channel_id=1, source_target_pairs={{0,30},{2,0},{4,2},{6,4},{8,6},{10,8},{12,10},{14,12},{16,14},{18,... | collective-permute-start | bytes 3080 | tf_op jit(solution)/shard_map/ppermute | solution.py:18
  12.3 1.3 %collective-permute-done.2.later_rows = f32[1,256]{1,0:T(1,128)S(1)} collective-permute-done((f32[1,256]{1,0:T(1,128)S(1)}, f32[1,256]{1,0:T(1,128)S(1)}, u32[]{:S(2)}, u32[]{:S(2)}) %collective-permute-start.2) | collective-permute-done | bytes 1056 | tf_op jit(solution)/shard_map/ppermute | solution.py:18
  13.6 5.2 %collective-permute-done.1.before_columns = f32[2,256]{1,0:T(2,128)S(1)} collective-permute-done((f32[2,256]{1,0:T(2,128)S(1)}, f32[2,256]{1,0:T(2,128)S(1)}, u32[]{:S(2)}, u32[]{:S(2)}) %collective-permute-start.1) | collective-permute-done | bytes 2080 | tf_op jit(solution)/shard_map/ppermute | solution.py:18
  18.9 0.0 collective-permute-done.earlier_texts
  18.9 0.0 collective-permute-start.3
  18.9 2.0 %shard_map.50 = (f32[32,1,128]{2,1,0:T(1,128)}, f32[256,256]{1,0:T(8,128)S(1)}, f32[1,256]{1,0:T(1,128)S(1)}) custom-call(bf16[3,256,1024]{2,1,0:T(8,128)(2,1)S(1)} %get-tuple-element.41.image_parts, f32[256,1024]{1,0:T(8,128)S(1)} %collective-permute-done.earlier_texts, f32[1,256]{1,0:T(1,128)S(1)} %get-tuple-element.39.self_rows, ...), custom_call_target="tpu_custom_call" | custom-call | flops 805306368 | bytes 4194304 | tf_op jit(solution)/shard_map/pallas_call | solution.py:273
  20.9 2.5 %collective-permute-start.4 = (f32[256,256]{1,0:T(8,128)S(1)}, f32[256,256]{1,0:T(8,128)S(1)}, u32[]{:S(2)}, u32[]{:S(2)}) collective-permute-start(f32[256,256]{1,0:T(8,128)S(1)} %get-tuple-element.57), channel_id=1, source_target_pairs={{0,30},{2,0},{4,2},{6,4},{8,6},{10,8},{12,10},{14,12},{16,14},{18,... | collective-permute-start | bytes 786440 | tf_op jit(solution)/shard_map/ppermute | solution.py:18
  23.4 2.7 %all-to-all-start = ((f32[32,1,128]{2,1,0:T(1,128)}), f32[32,1,128]{2,1,0:T(1,128)S(1)}, u32[]{:S(2)}, u32[]{:S(2)}) async-start(f32[32,1,128]{2,1,0:T(1,128)} %get-tuple-element.44), calls=%async_computation | async-start | bytes 32768 | tf_op jit(solution)/shard_map/all_to_all | solution.py:317
  26.1 3.4 %shard_map.51 = (f32[256,1024]{1,0:T(8,128)S(1)}, f32[256,1024]{1,0:T(8,128)S(1)}, bf16[3,256,1024]{2,1,0:T(8,128)(2,1)S(1)}, f32[256,256]{1,0:T(8,128)S(1)}) custom-call(f32[256,256]{1,0:T(8,128)S(1)} %get-tuple-element.47.weights, f32[256,1024]{1,0:T(8,128)S(1)} %collective-permute-done.earlier_texts, f32[1,256]{1,0:T(1,128)S(1)} %get-tuple-element.48.rows.rows_in, ...), custom_call_target="tpu_custom_call" | custom-call | flops 1610612736 | bytes 4194304 | tf_op jit(solution)/shard_map/pallas_call | solution.py:273
  29.4 0.0 collective-permute-done.3.first
  29.4 1.6 %shard_map.52 = (bf16[3,256,768]{2,1,0:T(8,128)(2,1)S(1)}, f32[256,256]{1,0:T(8,128)S(1)}, f32[256,1024]{1,0:T(8,128)S(1)}, f32[256,1024]{1,0:T(8,128)S(1)}) custom-call(bf16[3,256,1024]{2,1,0:T(8,128)(2,1)S(1)} %get-tuple-element.53.text_parts, f32[256,768]{1,0:T(8,128)S(1)} %collective-permute-done.3.first, f32[256,1024]{1,0:T(8,128)} %get-tuple-element.55.column_store, ...), custom_call_target="tpu_custom_call" | custom-call | flops 805306368 | bytes 4194304 | tf_op jit(solution)/shard_map/pallas_call | solution.py:273
  31.0 0.3 collective-permute-done.4.second
  31.3 3.9 %shard_map.53 = (f32[256,1024]{1,0:T(8,128)}, f32[256,1024]{1,0:T(8,128)}) custom-call(bf16[3,256,1024]{2,1,0:T(8,128)(2,1)S(1)} %get-tuple-element.53.text_parts, bf16[3,256,768]{2,1,0:T(8,128)(2,1)S(1)} %get-tuple-element.56.first_parts, f32[256,256]{1,0:T(8,128)S(1)} %collective-permute-done.4.second, f32[256,256]{1,0:T(8,128)S(1)} %get-tuple-element.58.product, ...), custom_call_target="tpu_custom_call" | custom-call | flops 2415919104 | bytes 4194304 | tf_op jit(solution)/shard_map/pallas_call | solution.py:273
  35.3 0.0 all-to-all-done.messages
  35.3 0.5 %shard_map.54 = f32[1,1]{1,0:T(1,128)} custom-call(f32[32,1,128]{2,1,0:T(1,128)S(1)} %all-to-all-done.messages), custom_call_target="tpu_custom_call" | custom-call | bytes 4194304 | tf_op jit(solution)/shard_map/pallas_call | solution.py:273
Async XLA Ops:
  0.6 18.2 %collective-permute-start = (f32[256,1024]{1,0:T(8,128)}, f32[256,1024]{1,0:T(8,128)S(1)}, u32[]{:S(2)}, u32[]{:S(2)}) collective-permute-start(f32[256,1024]{1,0:T(8,128)} %bitcast.7), channel_id=1, source_target_pairs={{0,2},{2,4},{4,6},{6,8},{8,10},{10,12},{12,14},{14,16},{16,18},{18... | collective-permute-start | bytes 3145736 | tf_op jit(solution)/shard_map/ppermute | solution.py:18
  7.2 11.6 %collective-permute-start.1 = (f32[2,256]{1,0:T(2,128)S(1)}, f32[2,256]{1,0:T(2,128)S(1)}, u32[]{:S(2)}, u32[]{:S(2)}) collective-permute-start(f32[2,256]{1,0:T(2,128)S(1)} %get-tuple-element.38.self_columns), channel_id=1, source_target_pairs={{0,2},{2,4},{4,6},{6,8},{8,10},{10,12},{12,14},{14,16},{16,18},{18... | collective-permute-start | bytes 6152 | tf_op jit(solution)/shard_map/ppermute | solution.py:18
  9.9 3.7 %collective-permute-start.2 = (f32[1,256]{1,0:T(1,128)S(1)}, f32[1,256]{1,0:T(1,128)S(1)}, u32[]{:S(2)}, u32[]{:S(2)}) collective-permute-start(f32[1,256]{1,0:T(1,128)S(1)} %get-tuple-element.39.self_rows), channel_id=1, source_target_pairs={{0,30},{2,0},{4,2},{6,4},{8,6},{10,8},{12,10},{14,12},{16,14},{18,... | collective-permute-start | bytes 3080 | tf_op jit(solution)/shard_map/ppermute | solution.py:18
  18.9 10.6 %collective-permute-start.3 = (f32[256,768]{1,0:T(8,128)S(1)}, f32[256,768]{1,0:T(8,128)S(1)}, u32[]{:S(2)}, u32[]{:S(2)}) collective-permute-start(f32[256,768]{1,0:T(8,128)S(1)} %get-tuple-element.54), channel_id=1, source_target_pairs={{0,30},{2,0},{4,2},{6,4},{8,6},{10,8},{12,10},{14,12},{16,14},{18,... | collective-permute-start | bytes 2359304 | tf_op jit(solution)/shard_map/ppermute | solution.py:18
  20.9 10.4 %collective-permute-start.4 = (f32[256,256]{1,0:T(8,128)S(1)}, f32[256,256]{1,0:T(8,128)S(1)}, u32[]{:S(2)}, u32[]{:S(2)}) collective-permute-start(f32[256,256]{1,0:T(8,128)S(1)} %get-tuple-element.57), channel_id=1, source_target_pairs={{0,30},{2,0},{4,2},{6,4},{8,6},{10,8},{12,10},{14,12},{16,14},{18,... | collective-permute-start | bytes 786440 | tf_op jit(solution)/shard_map/ppermute | solution.py:18
  23.4 11.9 %all-to-all-start = ((f32[32,1,128]{2,1,0:T(1,128)}), f32[32,1,128]{2,1,0:T(1,128)S(1)}, u32[]{:S(2)}, u32[]{:S(2)}) async-start(f32[32,1,128]{2,1,0:T(1,128)} %get-tuple-element.44), calls=%async_computation | async-start | bytes 32768 | tf_op jit(solution)/shard_map/all_to_all | solution.py:317

commit v7 on v6

--- a/solution.py
+++ b/solution.py
@@ -99,7 +99,7 @@
 
 def self_kernel(
     images, texts,
-    image_parts, row_part, columns_out, first, second, logits, image_store, text_store, row_product, column_term,
+    image_parts, row_part, columns_out, first, second, logits, text_store, row_product, column_term,
     own, image_in, text_in, text_parts, left, down, row_out, column_out, semaphores,
 ):
     copies = start([(images, image_in), (texts, text_in)], semaphores)
@@ -110,7 +110,7 @@
     second[...] = image_in[:, border:]
     copies[1].wait()
     store_parts(text_parts, text_in[...])
-    copies = start([(image_parts, image_store), (text_parts, text_store)], semaphores)
+    copies = start([(text_parts, text_store)], semaphores)
     block = logit_scale * rows_by_rows(image_parts, text_parts)
     count, width = text_in.shape
     diagonal = diagonal_mask(count)
@@ -129,7 +129,7 @@
         row_out[:, part] = rows_by_columns(left[...], text_parts.at[:, :, part])
         column_out[:, part] = rows_by_columns(down[...], image_parts.at[:, :, part])
 
-    copies += start([(row_out, row_product), (column_out, column_term), (own, logits)], semaphores.at[2:5])
+    copies += start([(row_out, row_product), (column_out, column_term), (own, logits)], semaphores.at[1:4])
     for copy in copies:
         copy.wait()
 
@@ -152,12 +152,12 @@
 
 
 def middle_kernel(
-    weights, earlier_texts, rows, self_rows, logits, image_store, text_store, row_store,
-    image_part, row_term, text_parts, own,
+    weights, earlier_texts, rows, self_rows, logits, images, text_store, row_store,
+    image_part, row_term, text_parts, own, own_images,
     earlier_parts, image_parts, row_product, left, down, semaphores,
 ):
     copies = start(
-        [(logits, own), (image_store, image_parts), (row_store, row_product), (text_store, text_parts)], semaphores
+        [(logits, own), (images, own_images), (row_store, row_product), (text_store, text_parts)], semaphores
     )
     count, width = image_part.shape
     diagonal = diagonal_mask(count)
@@ -175,6 +175,7 @@
     copies[0].wait()
     down[...] = left_parts(jnp.where(diagonal, 0.0, 0.5 * jnp.exp(own[...] - joint)).T)
     copies[1].wait()
+    store_parts(image_parts, own_images[...])
 
     @pl.loop(0, 2)
     def _(k):
@@ -186,12 +187,11 @@
     copies[3].wait()
 
 
-def first_kernel(text_parts, first, column_store, images, first_parts, product, column_term, own_images, semaphores):
-    copies = start([(column_store, column_term), (images, own_images)], semaphores)
+def first_kernel(text_parts, first, column_store, first_parts, product, column_term, semaphores):
+    (copy,) = start([(column_store, column_term)], semaphores)
     store_parts(first_parts, first[...])
     product[...] = rows_by_rows(text_parts.at[:, :, : first.shape[1]], first_parts)
-    for copy in copies:
-        copy.wait()
+    copy.wait()
 
 
 def last_kernel(
@@ -286,17 +286,17 @@
     devices = lax.axis_size("dp") * lax.axis_size("hst")
     earlier_texts = from_behind(texts, "dp", 1)
     (
-        image_parts, self_rows, self_columns, first, second, logits, image_store, text_store, row_product, column_term
+        image_parts, self_rows, self_columns, first, second, logits, text_store, row_product, column_term
     ) = call(
         self_kernel,
         3,
         [HB, HB],
         [
             (VM, *parts), (VM, *row), (VM, (2, count), f32),
-            (PV, (count, width - small), f32), (PV, (count, small), f32), (HB, *square), (HB, *parts), (HB, *parts), (HB, *whole), (HB, *whole),
+            (PV, (count, width - small), f32), (PV, (count, small), f32), (HB, *square), (HB, *parts), (HB, *whole), (HB, *whole),
         ],
         [square, whole, whole, parts, left, left, whole, whole],
-        6,
+        4,
     )(images, texts)
     before_columns = from_behind(self_columns, "dp", 1)
     later_rows = from_behind(self_rows, "dp", -1)
@@ -315,22 +315,22 @@
     second, weights = lax.optimization_barrier((second, weights))
     second = from_behind(second, "dp", -1)
     messages = lax.all_to_all(messages, ("dp", "hst"), 0, 0, tiled=True)
-    image_part, row_term, text_parts, logits = call(
+    image_part, row_term, text_parts, logits, own_images = call(
         middle_kernel,
         2,
         [VM] * 4 + [HB] * 4,
-        [(VM, *whole), (VM, *whole), (VM, *parts), (VM, *square)],
+        [(VM, *whole), (VM, *whole), (VM, *parts), (VM, *square), (VM, *whole)],
         [parts, parts, whole, left, left],
         4,
-    )(weights, earlier_texts, rows, self_rows, logits, image_store, text_store, row_product)
-    first_parts, product, column_term, images = call(
+    )(weights, earlier_texts, rows, self_rows, logits, images, text_store, row_product)
+    first_parts, product, column_term = call(
         first_kernel,
         1,
-        [VM, VM, HB, HB],
-        [(VM, (3, count, width - small), bf16), (VM, *square), (VM, *whole), (VM, *whole)],
+        [VM, VM, HB],
+        [(VM, (3, count, width - small), bf16), (VM, *square), (VM, *whole)],
         [],
-        2,
-    )(text_parts, first, column_term, images)
+        1,
+    )(text_parts, first, column_term)
     image_grads, text_grads = call(
         last_kernel,
         3,
@@ -339,7 +339,7 @@
         [parts, left, left, whole, whole],
         4,
     )(
-        text_parts, first_parts, second, product, logits, rows, later_rows, self_columns, image_part, row_term, column_term, images
+        text_parts, first_parts, second, product, logits, rows, later_rows, self_columns, image_part, row_term, column_term, own_images
     )
     messages, text_grads = lax.optimization_barrier((messages, text_grads))
     (mean_loss,) = call(functools.partial(loss_kernel, rows=count * devices), 0, [VM], [(VM, (1, 1), f32)], [], 0)(messages)

time: 36 us -> 36 us (level)
  no operation moved by 1% of the time
where the time goes in v7:
time: 36 us; the launch traced here: 35.8 us
  Pallas kernels  17.4 us (48%)
  starting transfers between devices  10.8 us (30%)
  waiting for transfers between devices  6.92 us (19%)
  between operations  0.7 us (2%)
    pallas_call x6, Pallas kernels, pinned(): run(*[pltpu.with_memory_space_constraint(v, pltpu.HBM) if spec is HB else...  17.4 us
    ppermute x5, starting transfers between devices, from_behind(): return lax.ppermute(value, axis, pairs)  8.1 us
    ppermute x5, waiting for transfers between devices, from_behind(): return lax.ppermute(value, axis, pairs)  6.92 us
    all_to_all x1, starting transfers between devices, on_device(): messages = lax.all_to_all(messages, ('dp', 'hst'), 0, 0, tiled=True)  2.69 us
  transfers between devices with their start and end apart: 6, of which 3 were waited for; matrix products, arithmetic and copies ran while one was open for 0% of the time, Pallas kernels for 47%

profile of v7, /device:TPU:0, one launch (start us, length us, event | category | flops | bytes accessed | tf_op | source)
XLA Modules:
  0.0 35.8 jit_solution(10615746250098375832)
XLA Ops:
  0.6 0.5 %collective-permute-start = (f32[256,1024]{1,0:T(8,128)}, f32[256,1024]{1,0:T(8,128)S(1)}, u32[]{:S(2)}, u32[]{:S(2)}) collective-permute-start(f32[256,1024]{1,0:T(8,128)} %bitcast.5), channel_id=1, source_target_pairs={{0,2},{2,4},{4,6},{6,8},{8,10},{10,12},{12,14},{14,16},{16,18},{18... | collective-permute-start | bytes 3145736 | tf_op jit(solution)/shard_map/ppermute | solution.py:18
  1.1 6.0 %shard_map.49 = (bf16[3,256,1024]{2,1,0:T(8,128)(2,1)S(1)}, f32[1,256]{1,0:T(1,128)S(1)}, f32[2,256]{1,0:T(2,128)S(1)}, f32[256,768]{1,0:T(8,128)S(1)}, f32[256,...) custom-call(f32[256,1024]{1,0:T(8,128)} %bitcast.7, ...), custom_call_target="tpu_custom_call" | custom-call | flops 2415919104 | bytes 4194304 | tf_op jit(solution)/shard_map/pallas_call | solution.py:273
  7.2 2.7 %collective-permute-start.1 = (f32[2,256]{1,0:T(2,128)S(1)}, f32[2,256]{1,0:T(2,128)S(1)}, u32[]{:S(2)}, u32[]{:S(2)}) collective-permute-start(f32[2,256]{1,0:T(2,128)S(1)} %get-tuple-element.37.self_columns), channel_id=1, source_target_pairs={{0,2},{2,4},{4,6},{6,8},{8,10},{10,12},{12,14},{14,16},{16,18},{18... | collective-permute-start | bytes 6152 | tf_op jit(solution)/shard_map/ppermute | solution.py:18
  9.9 2.4 %collective-permute-start.2 = (f32[1,256]{1,0:T(1,128)S(1)}, f32[1,256]{1,0:T(1,128)S(1)}, u32[]{:S(2)}, u32[]{:S(2)}) collective-permute-start(f32[1,256]{1,0:T(1,128)S(1)} %get-tuple-element.38.self_rows), channel_id=1, source_target_pairs={{0,30},{2,0},{4,2},{6,4},{8,6},{10,8},{12,10},{14,12},{16,14},{18,... | collective-permute-start | bytes 3080 | tf_op jit(solution)/shard_map/ppermute | solution.py:18
  12.3 1.3 %collective-permute-done.2.later_rows = f32[1,256]{1,0:T(1,128)S(1)} collective-permute-done((f32[1,256]{1,0:T(1,128)S(1)}, f32[1,256]{1,0:T(1,128)S(1)}, u32[]{:S(2)}, u32[]{:S(2)}) %collective-permute-start.2) | collective-permute-done | bytes 1056 | tf_op jit(solution)/shard_map/ppermute | solution.py:18
  13.6 5.3 %collective-permute-done.1.before_columns = f32[2,256]{1,0:T(2,128)S(1)} collective-permute-done((f32[2,256]{1,0:T(2,128)S(1)}, f32[2,256]{1,0:T(2,128)S(1)}, u32[]{:S(2)}, u32[]{:S(2)}) %collective-permute-start.1) | collective-permute-done | bytes 2080 | tf_op jit(solution)/shard_map/ppermute | solution.py:18
  18.9 0.0 collective-permute-done.earlier_texts
  18.9 0.0 collective-permute-start.3
  18.9 2.0 %shard_map.50 = (f32[32,1,128]{2,1,0:T(1,128)}, f32[256,256]{1,0:T(8,128)S(1)}, f32[1,256]{1,0:T(1,128)S(1)}) custom-call(bf16[3,256,1024]{2,1,0:T(8,128)(2,1)S(1)} %get-tuple-element.40.image_parts, f32[256,1024]{1,0:T(8,128)S(1)} %collective-permute-done.earlier_texts, f32[1,256]{1,0:T(1,128)S(1)} %get-tuple-element.38.self_rows, ...), custom_call_target="tpu_custom_call" | custom-call | flops 805306368 | bytes 4194304 | tf_op jit(solution)/shard_map/pallas_call | solution.py:273
  20.9 2.5 %collective-permute-start.4 = (f32[256,256]{1,0:T(8,128)S(1)}, f32[256,256]{1,0:T(8,128)S(1)}, u32[]{:S(2)}, u32[]{:S(2)}) collective-permute-start(f32[256,256]{1,0:T(8,128)S(1)} %get-tuple-element.55), channel_id=1, source_target_pairs={{0,30},{2,0},{4,2},{6,4},{8,6},{10,8},{12,10},{14,12},{16,14},{18,... | collective-permute-start | bytes 786440 | tf_op jit(solution)/shard_map/ppermute | solution.py:18
  23.4 2.7 %all-to-all-start = ((f32[32,1,128]{2,1,0:T(1,128)}), f32[32,1,128]{2,1,0:T(1,128)S(1)}, u32[]{:S(2)}, u32[]{:S(2)}) async-start(f32[32,1,128]{2,1,0:T(1,128)} %get-tuple-element.43), calls=%async_computation | async-start | bytes 32768 | tf_op jit(solution)/shard_map/all_to_all | solution.py:317
  26.1 3.6 %shard_map.51 = (f32[256,1024]{1,0:T(8,128)S(1)}, f32[256,1024]{1,0:T(8,128)S(1)}, bf16[3,256,1024]{2,1,0:T(8,128)(2,1)S(1)}, f32[256,256]{1,0:T(8,128)S(1)}, f32[256,1024]{1,0:T(8,128)S(1)}) custom-call(f32[256,256]{1,0:T(8,128)S(1)} %get-tuple-element.46.weights, f32[256,1024]{1,0:T(8,128)S(1)} %collective-permute-done.earlier_texts, ...), custom_call_target="tpu_custom_call" | custom-call | flops 1610612736 | bytes 4194304 | tf_op jit(solution)/shard_map/pallas_call | solution.py:273
  29.7 0.0 collective-permute-done.3.first
  29.7 1.2 %shard_map.52 = (bf16[3,256,768]{2,1,0:T(8,128)(2,1)S(1)}, f32[256,256]{1,0:T(8,128)S(1)}, f32[256,1024]{1,0:T(8,128)S(1)}) custom-call(bf16[3,256,1024]{2,1,0:T(8,128)(2,1)S(1)} %get-tuple-element.51.text_parts, f32[256,768]{1,0:T(8,128)S(1)} %collective-permute-done.3.first, f32[256,1024]{1,0:T(8,128)} %get-tuple-element.53.column_store), custom_call_target="tpu_custom_call" | custom-call | flops 805306368 | bytes 4194304 | tf_op jit(solution)/shard_map/pallas_call | solution.py:273
  31.0 0.4 %collective-permute-done.4.second = f32[256,256]{1,0:T(8,128)S(1)} collective-permute-done((f32[256,256]{1,0:T(8,128)S(1)}, f32[256,256]{1,0:T(8,128)S(1)}, u32[]{:S(2)}, u32[]{:S(2)}) %collective-permute-start.4) | collective-permute-done | bytes 262176 | tf_op jit(solution)/shard_map/ppermute | solution.py:18
  31.3 3.9 %shard_map.53 = (f32[256,1024]{1,0:T(8,128)}, f32[256,1024]{1,0:T(8,128)}) custom-call(bf16[3,256,1024]{2,1,0:T(8,128)(2,1)S(1)} %get-tuple-element.51.text_parts, bf16[3,256,768]{2,1,0:T(8,128)(2,1)S(1)} %get-tuple-element.54.first_parts, f32[256,256]{1,0:T(8,128)S(1)} %collective-permute-done.4.second, f32[256,256]{1,0:T(8,128)S(1)} %get-tuple-element.56.product, ...), custom_call_target="tpu_custom_call" | custom-call | flops 2415919104 | bytes 4194304 | tf_op jit(solution)/shard_map/pallas_call | solution.py:273
  35.3 0.0 all-to-all-done.messages
  35.3 0.5 %shard_map.54 = f32[1,1]{1,0:T(1,128)} custom-call(f32[32,1,128]{2,1,0:T(1,128)S(1)} %all-to-all-done.messages), custom_call_target="tpu_custom_call" | custom-call | bytes 4194304 | tf_op jit(solution)/shard_map/pallas_call | solution.py:273
Async XLA Ops:
  0.6 18.2 %collective-permute-start = (f32[256,1024]{1,0:T(8,128)}, f32[256,1024]{1,0:T(8,128)S(1)}, u32[]{:S(2)}, u32[]{:S(2)}) collective-permute-start(f32[256,1024]{1,0:T(8,128)} %bitcast.5), channel_id=1, source_target_pairs={{0,2},{2,4},{4,6},{6,8},{8,10},{10,12},{12,14},{14,16},{16,18},{18... | collective-permute-start | bytes 3145736 | tf_op jit(solution)/shard_map/ppermute | solution.py:18
  7.2 11.7 %collective-permute-start.1 = (f32[2,256]{1,0:T(2,128)S(1)}, f32[2,256]{1,0:T(2,128)S(1)}, u32[]{:S(2)}, u32[]{:S(2)}) collective-permute-start(f32[2,256]{1,0:T(2,128)S(1)} %get-tuple-element.37.self_columns), channel_id=1, source_target_pairs={{0,2},{2,4},{4,6},{6,8},{8,10},{10,12},{12,14},{14,16},{16,18},{18... | collective-permute-start | bytes 6152 | tf_op jit(solution)/shard_map/ppermute | solution.py:18
  9.9 3.7 %collective-permute-start.2 = (f32[1,256]{1,0:T(1,128)S(1)}, f32[1,256]{1,0:T(1,128)S(1)}, u32[]{:S(2)}, u32[]{:S(2)}) collective-permute-start(f32[1,256]{1,0:T(1,128)S(1)} %get-tuple-element.38.self_rows), channel_id=1, source_target_pairs={{0,30},{2,0},{4,2},{6,4},{8,6},{10,8},{12,10},{14,12},{16,14},{18,... | collective-permute-start | bytes 3080 | tf_op jit(solution)/shard_map/ppermute | solution.py:18
  18.9 10.9 %collective-permute-start.3 = (f32[256,768]{1,0:T(8,128)S(1)}, f32[256,768]{1,0:T(8,128)S(1)}, u32[]{:S(2)}, u32[]{:S(2)}) collective-permute-start(f32[256,768]{1,0:T(8,128)S(1)} %get-tuple-element.52), channel_id=1, source_target_pairs={{0,30},{2,0},{4,2},{6,4},{8,6},{10,8},{12,10},{14,12},{16,14},{18,... | collective-permute-start | bytes 2359304 | tf_op jit(solution)/shard_map/ppermute | solution.py:18
  20.9 10.4 %collective-permute-start.4 = (f32[256,256]{1,0:T(8,128)S(1)}, f32[256,256]{1,0:T(8,128)S(1)}, u32[]{:S(2)}, u32[]{:S(2)}) collective-permute-start(f32[256,256]{1,0:T(8,128)S(1)} %get-tuple-element.55), channel_id=1, source_target_pairs={{0,30},{2,0},{4,2},{6,4},{8,6},{10,8},{12,10},{14,12},{16,14},{18,... | collective-permute-start | bytes 786440 | tf_op jit(solution)/shard_map/ppermute | solution.py:18
  23.4 11.9 %all-to-all-start = ((f32[32,1,128]{2,1,0:T(1,128)}), f32[32,1,128]{2,1,0:T(1,128)S(1)}, u32[]{:S(2)}, u32[]{:S(2)}) async-start(f32[32,1,128]{2,1,0:T(1,128)} %get-tuple-element.43), calls=%async_computation | async-start | bytes 32768 | tf_op jit(solution)/shard_map/all_to_all | solution.py:317

commit v8 on v7

--- a/solution.py
+++ b/solution.py
@@ -224,7 +224,7 @@
             pltpu.make_async_copy(text_out.at[:, part], text_grads.at[:, part], semaphores.at[2 * k + 1]),
         )
 
-    @pl.loop(0, 2)
+    @pl.loop(0, 2, unroll=True)
     def _(k):
         part = columns_at(k, half)
         of_image, of_text = copies(k)

time: 36 us -> 36 us (level)
  no operation moved by 1% of the time
where the time goes in v8:
time: 36 us; the launch traced here: 35.8 us
  Pallas kernels  17.4 us (48%)
  starting transfers between devices  10.8 us (30%)
  waiting for transfers between devices  6.92 us (19%)
  between operations  0.7 us (2%)
    pallas_call x6, Pallas kernels, pinned(): run(*[pltpu.with_memory_space_constraint(v, pltpu.HBM) if spec is HB else...  17.4 us
    ppermute x5, starting transfers between devices, from_behind(): return lax.ppermute(value, axis, pairs)  8.1 us
    ppermute x5, waiting for transfers between devices, from_behind(): return lax.ppermute(value, axis, pairs)  6.92 us
    all_to_all x1, starting transfers between devices, on_device(): messages = lax.all_to_all(messages, ('dp', 'hst'), 0, 0, tiled=True)  2.69 us
  transfers between devices with their start and end apart: 6, of which 3 were waited for; matrix products, arithmetic and copies ran while one was open for 0% of the time, Pallas kernels for 47%

profile of v8, /device:TPU:0, one launch (start us, length us, event | category | flops | bytes accessed | tf_op | source)
XLA Modules:
  0.0 35.8 jit_solution(7301016804892059029)
XLA Ops:
  0.6 0.5 %collective-permute-start = (f32[256,1024]{1,0:T(8,128)}, f32[256,1024]{1,0:T(8,128)S(1)}, u32[]{:S(2)}, u32[]{:S(2)}) collective-permute-start(f32[256,1024]{1,0:T(8,128)} %bitcast.5), channel_id=1, source_target_pairs={{0,2},{2,4},{4,6},{6,8},{8,10},{10,12},{12,14},{14,16},{16,18},{18... | collective-permute-start | bytes 3145736 | tf_op jit(solution)/shard_map/ppermute | solution.py:18
  1.1 6.0 %shard_map.49 = (bf16[3,256,1024]{2,1,0:T(8,128)(2,1)S(1)}, f32[1,256]{1,0:T(1,128)S(1)}, f32[2,256]{1,0:T(2,128)S(1)}, f32[256,768]{1,0:T(8,128)S(1)}, f32[256,...) custom-call(f32[256,1024]{1,0:T(8,128)} %bitcast.7, ...), custom_call_target="tpu_custom_call" | custom-call | flops 2415919104 | bytes 4194304 | tf_op jit(solution)/shard_map/pallas_call | solution.py:273
  7.2 2.7 %collective-permute-start.1 = (f32[2,256]{1,0:T(2,128)S(1)}, f32[2,256]{1,0:T(2,128)S(1)}, u32[]{:S(2)}, u32[]{:S(2)}) collective-permute-start(f32[2,256]{1,0:T(2,128)S(1)} %get-tuple-element.37.self_columns), channel_id=1, source_target_pairs={{0,2},{2,4},{4,6},{6,8},{8,10},{10,12},{12,14},{14,16},{16,18},{18... | collective-permute-start | bytes 6152 | tf_op jit(solution)/shard_map/ppermute | solution.py:18
  9.9 2.4 %collective-permute-start.2 = (f32[1,256]{1,0:T(1,128)S(1)}, f32[1,256]{1,0:T(1,128)S(1)}, u32[]{:S(2)}, u32[]{:S(2)}) collective-permute-start(f32[1,256]{1,0:T(1,128)S(1)} %get-tuple-element.38.self_rows), channel_id=1, source_target_pairs={{0,30},{2,0},{4,2},{6,4},{8,6},{10,8},{12,10},{14,12},{16,14},{18,... | collective-permute-start | bytes 3080 | tf_op jit(solution)/shard_map/ppermute | solution.py:18
  12.3 1.3 %collective-permute-done.2.later_rows = f32[1,256]{1,0:T(1,128)S(1)} collective-permute-done((f32[1,256]{1,0:T(1,128)S(1)}, f32[1,256]{1,0:T(1,128)S(1)}, u32[]{:S(2)}, u32[]{:S(2)}) %collective-permute-start.2) | collective-permute-done | bytes 1056 | tf_op jit(solution)/shard_map/ppermute | solution.py:18
  13.6 5.3 %collective-permute-done.1.before_columns = f32[2,256]{1,0:T(2,128)S(1)} collective-permute-done((f32[2,256]{1,0:T(2,128)S(1)}, f32[2,256]{1,0:T(2,128)S(1)}, u32[]{:S(2)}, u32[]{:S(2)}) %collective-permute-start.1) | collective-permute-done | bytes 2080 | tf_op jit(solution)/shard_map/ppermute | solution.py:18
  18.9 0.0 collective-permute-done.earlier_texts
  18.9 0.0 collective-permute-start.3
  18.9 2.0 %shard_map.50 = (f32[32,1,128]{2,1,0:T(1,128)}, f32[256,256]{1,0:T(8,128)S(1)}, f32[1,256]{1,0:T(1,128)S(1)}) custom-call(bf16[3,256,1024]{2,1,0:T(8,128)(2,1)S(1)} %get-tuple-element.40.image_parts, f32[256,1024]{1,0:T(8,128)S(1)} %collective-permute-done.earlier_texts, f32[1,256]{1,0:T(1,128)S(1)} %get-tuple-element.38.self_rows, ...), custom_call_target="tpu_custom_call" | custom-call | flops 805306368 | bytes 4194304 | tf_op jit(solution)/shard_map/pallas_call | solution.py:273
  20.9 2.5 %collective-permute-start.4 = (f32[256,256]{1,0:T(8,128)S(1)}, f32[256,256]{1,0:T(8,128)S(1)}, u32[]{:S(2)}, u32[]{:S(2)}) collective-permute-start(f32[256,256]{1,0:T(8,128)S(1)} %get-tuple-element.55), channel_id=1, source_target_pairs={{0,30},{2,0},{4,2},{6,4},{8,6},{10,8},{12,10},{14,12},{16,14},{18,... | collective-permute-start | bytes 786440 | tf_op jit(solution)/shard_map/ppermute | solution.py:18
  23.4 2.7 %all-to-all-start = ((f32[32,1,128]{2,1,0:T(1,128)}), f32[32,1,128]{2,1,0:T(1,128)S(1)}, u32[]{:S(2)}, u32[]{:S(2)}) async-start(f32[32,1,128]{2,1,0:T(1,128)} %get-tuple-element.43), calls=%async_computation | async-start | bytes 32768 | tf_op jit(solution)/shard_map/all_to_all | solution.py:317
  26.1 3.6 %shard_map.51 = (f32[256,1024]{1,0:T(8,128)S(1)}, f32[256,1024]{1,0:T(8,128)S(1)}, bf16[3,256,1024]{2,1,0:T(8,128)(2,1)S(1)}, f32[256,256]{1,0:T(8,128)S(1)}, f32[256,1024]{1,0:T(8,128)S(1)}) custom-call(f32[256,256]{1,0:T(8,128)S(1)} %get-tuple-element.46.weights, f32[256,1024]{1,0:T(8,128)S(1)} %collective-permute-done.earlier_texts, ...), custom_call_target="tpu_custom_call" | custom-call | flops 1610612736 | bytes 4194304 | tf_op jit(solution)/shard_map/pallas_call | solution.py:273
  29.7 0.0 collective-permute-done.3.first
  29.7 1.2 %shard_map.52 = (bf16[3,256,768]{2,1,0:T(8,128)(2,1)S(1)}, f32[256,256]{1,0:T(8,128)S(1)}, f32[256,1024]{1,0:T(8,128)S(1)}) custom-call(bf16[3,256,1024]{2,1,0:T(8,128)(2,1)S(1)} %get-tuple-element.51.text_parts, f32[256,768]{1,0:T(8,128)S(1)} %collective-permute-done.3.first, f32[256,1024]{1,0:T(8,128)} %get-tuple-element.53.column_store), custom_call_target="tpu_custom_call" | custom-call | flops 805306368 | bytes 4194304 | tf_op jit(solution)/shard_map/pallas_call | solution.py:273
  31.0 0.4 %collective-permute-done.4.second = f32[256,256]{1,0:T(8,128)S(1)} collective-permute-done((f32[256,256]{1,0:T(8,128)S(1)}, f32[256,256]{1,0:T(8,128)S(1)}, u32[]{:S(2)}, u32[]{:S(2)}) %collective-permute-start.4) | collective-permute-done | bytes 262176 | tf_op jit(solution)/shard_map/ppermute | solution.py:18
  31.3 3.9 %shard_map.53 = (f32[256,1024]{1,0:T(8,128)}, f32[256,1024]{1,0:T(8,128)}) custom-call(bf16[3,256,1024]{2,1,0:T(8,128)(2,1)S(1)} %get-tuple-element.51.text_parts, bf16[3,256,768]{2,1,0:T(8,128)(2,1)S(1)} %get-tuple-element.54.first_parts, f32[256,256]{1,0:T(8,128)S(1)} %collective-permute-done.4.second, f32[256,256]{1,0:T(8,128)S(1)} %get-tuple-element.56.product, ...), custom_call_target="tpu_custom_call" | custom-call | flops 2415919104 | bytes 4194304 | tf_op jit(solution)/shard_map/pallas_call | solution.py:273
  35.3 0.0 all-to-all-done.messages
  35.3 0.5 %shard_map.54 = f32[1,1]{1,0:T(1,128)} custom-call(f32[32,1,128]{2,1,0:T(1,128)S(1)} %all-to-all-done.messages), custom_call_target="tpu_custom_call" | custom-call | bytes 4194304 | tf_op jit(solution)/shard_map/pallas_call | solution.py:273
Async XLA Ops:
  0.6 18.2 %collective-permute-start = (f32[256,1024]{1,0:T(8,128)}, f32[256,1024]{1,0:T(8,128)S(1)}, u32[]{:S(2)}, u32[]{:S(2)}) collective-permute-start(f32[256,1024]{1,0:T(8,128)} %bitcast.5), channel_id=1, source_target_pairs={{0,2},{2,4},{4,6},{6,8},{8,10},{10,12},{12,14},{14,16},{16,18},{18... | collective-permute-start | bytes 3145736 | tf_op jit(solution)/shard_map/ppermute | solution.py:18
  7.2 11.7 %collective-permute-start.1 = (f32[2,256]{1,0:T(2,128)S(1)}, f32[2,256]{1,0:T(2,128)S(1)}, u32[]{:S(2)}, u32[]{:S(2)}) collective-permute-start(f32[2,256]{1,0:T(2,128)S(1)} %get-tuple-element.37.self_columns), channel_id=1, source_target_pairs={{0,2},{2,4},{4,6},{6,8},{8,10},{10,12},{12,14},{14,16},{16,18},{18... | collective-permute-start | bytes 6152 | tf_op jit(solution)/shard_map/ppermute | solution.py:18
  9.9 3.7 %collective-permute-start.2 = (f32[1,256]{1,0:T(1,128)S(1)}, f32[1,256]{1,0:T(1,128)S(1)}, u32[]{:S(2)}, u32[]{:S(2)}) collective-permute-start(f32[1,256]{1,0:T(1,128)S(1)} %get-tuple-element.38.self_rows), channel_id=1, source_target_pairs={{0,30},{2,0},{4,2},{6,4},{8,6},{10,8},{12,10},{14,12},{16,14},{18,... | collective-permute-start | bytes 3080 | tf_op jit(solution)/shard_map/ppermute | solution.py:18
  18.9 10.9 %collective-permute-start.3 = (f32[256,768]{1,0:T(8,128)S(1)}, f32[256,768]{1,0:T(8,128)S(1)}, u32[]{:S(2)}, u32[]{:S(2)}) collective-permute-start(f32[256,768]{1,0:T(8,128)S(1)} %get-tuple-element.52), channel_id=1, source_target_pairs={{0,30},{2,0},{4,2},{6,4},{8,6},{10,8},{12,10},{14,12},{16,14},{18,... | collective-permute-start | bytes 2359304 | tf_op jit(solution)/shard_map/ppermute | solution.py:18
  20.9 10.4 %collective-permute-start.4 = (f32[256,256]{1,0:T(8,128)S(1)}, f32[256,256]{1,0:T(8,128)S(1)}, u32[]{:S(2)}, u32[]{:S(2)}) collective-permute-start(f32[256,256]{1,0:T(8,128)S(1)} %get-tuple-element.55), channel_id=1, source_target_pairs={{0,30},{2,0},{4,2},{6,4},{8,6},{10,8},{12,10},{14,12},{16,14},{18,... | collective-permute-start | bytes 786440 | tf_op jit(solution)/shard_map/ppermute | solution.py:18
  23.4 11.9 %all-to-all-start = ((f32[32,1,128]{2,1,0:T(1,128)}), f32[32,1,128]{2,1,0:T(1,128)S(1)}, u32[]{:S(2)}, u32[]{:S(2)}) async-start(f32[32,1,128]{2,1,0:T(1,128)} %get-tuple-element.43), calls=%async_computation | async-start | bytes 32768 | tf_op jit(solution)/shard_map/all_to_all | solution.py:317

commit v9 on v8

--- a/solution.py
+++ b/solution.py
@@ -161,7 +161,7 @@
     )
     count, width = image_part.shape
     diagonal = diagonal_mask(count)
-    left[...] = left_parts(weights[...])
+    left[...] = left_parts(logit_scale * weights[...])
     store_parts(earlier_parts, earlier_texts[...])
     joint = as_column(rows[...], diagonal)
     scale = as_column(jnp.exp(self_rows[...] - rows[...]), diagonal)
@@ -173,7 +173,7 @@
         image_part[:, part] = rows_by_columns(left[...], earlier_parts.at[:, :, part])
 
     copies[0].wait()
-    down[...] = left_parts(jnp.where(diagonal, 0.0, 0.5 * jnp.exp(own[...] - joint)).T)
+    down[...] = left_parts(jnp.where(diagonal, 0.0, (0.5 * logit_scale) * jnp.exp(own[...] - joint)).T)
     copies[1].wait()
     store_parts(image_parts, own_images[...])
 
@@ -183,7 +183,7 @@
         row_term[:, part] = rows_by_columns(down[...], image_parts.at[:, :, part])
 
     copies[2].wait()
-    image_part[...] += scale * row_product[...]
+    image_part[...] += (logit_scale * scale) * row_product[...]
     copies[3].wait()
 
 
@@ -209,12 +209,12 @@
     own_columns = as_column(self_columns[0:1, :], diagonal)
     rows, by_rows = joint_logsum(block, later_rows[...], 0)
     columns, by_columns = joint_logsum(block, own_columns, 1)
-    left[...] = left_parts(by_rows + by_columns)
+    left[...] = left_parts(logit_scale * (by_rows + by_columns))
     across, positive = as_row(columns, diagonal), self_columns[1:2, :]
     own = 0.5 * (jnp.exp(positive - rows_in[...]) + jnp.exp(positive - across)) - 1.0
-    own_left[...] = left_parts(jnp.where(diagonal, own, 0.5 * jnp.exp(logits[...] - across)))
-    own_down = as_column(own, diagonal)
-    scale = jnp.exp(own_columns - columns)
+    own_left[...] = left_parts(logit_scale * jnp.where(diagonal, own, 0.5 * jnp.exp(logits[...] - across)))
+    own_down = logit_scale * as_column(own, diagonal)
+    scale = logit_scale * jnp.exp(own_columns - columns)
     half = width // 2
 
     def copies(k):
@@ -229,11 +229,11 @@
         part = columns_at(k, half)
         of_image, of_text = copies(k)
         terms = rows_by_columns(own_left[...], text_parts.at[:, :, part])
-        image_out[:, part] = logit_scale * (image_part[:, part] + terms)
+        image_out[:, part] = image_part[:, part] + terms
         of_image.start()
         terms = rows_by_columns(left[...], later_parts.at[:, :, part])
         own_terms = row_term[:, part] + scale * column_term[:, part] + own_down * image_in[:, part]
-        text_out[:, part] = logit_scale * (own_terms + terms)
+        text_out[:, part] = own_terms + terms
         of_text.start()
 
     for k in range(2):

time: 36 us -> 36 us (level)
  no operation moved by 1% of the time
where the time goes in v9:
time: 36 us; the launch traced here: 35.8 us
  Pallas kernels  17.4 us (48%)
  starting transfers between devices  10.8 us (30%)
  waiting for transfers between devices  6.89 us (19%)
  between operations  0.7 us (2%)
    pallas_call x6, Pallas kernels, pinned(): run(*[pltpu.with_memory_space_constraint(v, pltpu.HBM) if spec is HB else...  17.4 us
    ppermute x5, starting transfers between devices, from_behind(): return lax.ppermute(value, axis, pairs)  8.1 us
    ppermute x5, waiting for transfers between devices, from_behind(): return lax.ppermute(value, axis, pairs)  6.89 us
    all_to_all x1, starting transfers between devices, on_device(): messages = lax.all_to_all(messages, ('dp', 'hst'), 0, 0, tiled=True)  2.69 us
  transfers between devices with their start and end apart: 6, of which 3 were waited for; matrix products, arithmetic and copies ran while one was open for 0% of the time, Pallas kernels for 47%

profile of v9, /device:TPU:0, one launch (start us, length us, event | category | flops | bytes accessed | tf_op | source)
XLA Modules:
  0.0 35.8 jit_solution(12526166532802901908)
XLA Ops:
  0.6 0.5 %collective-permute-start = (f32[256,1024]{1,0:T(8,128)}, f32[256,1024]{1,0:T(8,128)S(1)}, u32[]{:S(2)}, u32[]{:S(2)}) collective-permute-start(f32[256,1024]{1,0:T(8,128)} %bitcast.5), channel_id=1, source_target_pairs={{0,2},{2,4},{4,6},{6,8},{8,10},{10,12},{12,14},{14,16},{16,18},{18... | collective-permute-start | bytes 3145736 | tf_op jit(solution)/shard_map/ppermute | solution.py:18
  1.1 6.0 %shard_map.49 = (bf16[3,256,1024]{2,1,0:T(8,128)(2,1)S(1)}, f32[1,256]{1,0:T(1,128)S(1)}, f32[2,256]{1,0:T(2,128)S(1)}, f32[256,768]{1,0:T(8,128)S(1)}, f32[256,...) custom-call(f32[256,1024]{1,0:T(8,128)} %bitcast.7, ...), custom_call_target="tpu_custom_call" | custom-call | flops 2415919104 | bytes 4194304 | tf_op jit(solution)/shard_map/pallas_call | solution.py:273
  7.2 2.7 %collective-permute-start.1 = (f32[2,256]{1,0:T(2,128)S(1)}, f32[2,256]{1,0:T(2,128)S(1)}, u32[]{:S(2)}, u32[]{:S(2)}) collective-permute-start(f32[2,256]{1,0:T(2,128)S(1)} %get-tuple-element.37.self_columns), channel_id=1, source_target_pairs={{0,2},{2,4},{4,6},{6,8},{8,10},{10,12},{12,14},{14,16},{16,18},{18... | collective-permute-start | bytes 6152 | tf_op jit(solution)/shard_map/ppermute | solution.py:18
  9.9 2.4 %collective-permute-start.2 = (f32[1,256]{1,0:T(1,128)S(1)}, f32[1,256]{1,0:T(1,128)S(1)}, u32[]{:S(2)}, u32[]{:S(2)}) collective-permute-start(f32[1,256]{1,0:T(1,128)S(1)} %get-tuple-element.38.self_rows), channel_id=1, source_target_pairs={{0,30},{2,0},{4,2},{6,4},{8,6},{10,8},{12,10},{14,12},{16,14},{18,... | collective-permute-start | bytes 3080 | tf_op jit(solution)/shard_map/ppermute | solution.py:18
  12.3 1.3 %collective-permute-done.2.later_rows = f32[1,256]{1,0:T(1,128)S(1)} collective-permute-done((f32[1,256]{1,0:T(1,128)S(1)}, f32[1,256]{1,0:T(1,128)S(1)}, u32[]{:S(2)}, u32[]{:S(2)}) %collective-permute-start.2) | collective-permute-done | bytes 1056 | tf_op jit(solution)/shard_map/ppermute | solution.py:18
  13.6 5.3 %collective-permute-done.1.before_columns = f32[2,256]{1,0:T(2,128)S(1)} collective-permute-done((f32[2,256]{1,0:T(2,128)S(1)}, f32[2,256]{1,0:T(2,128)S(1)}, u32[]{:S(2)}, u32[]{:S(2)}) %collective-permute-start.1) | collective-permute-done | bytes 2080 | tf_op jit(solution)/shard_map/ppermute | solution.py:18
  18.9 0.0 collective-permute-done.earlier_texts
  18.9 0.0 collective-permute-start.3
  18.9 2.0 %shard_map.50 = (f32[32,1,128]{2,1,0:T(1,128)}, f32[256,256]{1,0:T(8,128)S(1)}, f32[1,256]{1,0:T(1,128)S(1)}) custom-call(bf16[3,256,1024]{2,1,0:T(8,128)(2,1)S(1)} %get-tuple-element.40.image_parts, f32[256,1024]{1,0:T(8,128)S(1)} %collective-permute-done.earlier_texts, f32[1,256]{1,0:T(1,128)S(1)} %get-tuple-element.38.self_rows, ...), custom_call_target="tpu_custom_call" | custom-call | flops 805306368 | bytes 4194304 | tf_op jit(solution)/shard_map/pallas_call | solution.py:273
  20.9 2.5 %collective-permute-start.4 = (f32[256,256]{1,0:T(8,128)S(1)}, f32[256,256]{1,0:T(8,128)S(1)}, u32[]{:S(2)}, u32[]{:S(2)}) collective-permute-start(f32[256,256]{1,0:T(8,128)S(1)} %get-tuple-element.55), channel_id=1, source_target_pairs={{0,30},{2,0},{4,2},{6,4},{8,6},{10,8},{12,10},{14,12},{16,14},{18,... | collective-permute-start | bytes 786440 | tf_op jit(solution)/shard_map/ppermute | solution.py:18
  23.4 2.7 %all-to-all-start = ((f32[32,1,128]{2,1,0:T(1,128)}), f32[32,1,128]{2,1,0:T(1,128)S(1)}, u32[]{:S(2)}, u32[]{:S(2)}) async-start(f32[32,1,128]{2,1,0:T(1,128)} %get-tuple-element.43), calls=%async_computation | async-start | bytes 32768 | tf_op jit(solution)/shard_map/all_to_all | solution.py:317
  26.1 3.7 %shard_map.51 = (f32[256,1024]{1,0:T(8,128)S(1)}, f32[256,1024]{1,0:T(8,128)S(1)}, bf16[3,256,1024]{2,1,0:T(8,128)(2,1)S(1)}, f32[256,256]{1,0:T(8,128)S(1)}, f32[256,1024]{1,0:T(8,128)S(1)}) custom-call(f32[256,256]{1,0:T(8,128)S(1)} %get-tuple-element.46.weights, f32[256,1024]{1,0:T(8,128)S(1)} %collective-permute-done.earlier_texts, ...), custom_call_target="tpu_custom_call" | custom-call | flops 1610612736 | bytes 4194304 | tf_op jit(solution)/shard_map/pallas_call | solution.py:273
  29.7 0.0 collective-permute-done.3.first
  29.8 1.2 %shard_map.52 = (bf16[3,256,768]{2,1,0:T(8,128)(2,1)S(1)}, f32[256,256]{1,0:T(8,128)S(1)}, f32[256,1024]{1,0:T(8,128)S(1)}) custom-call(bf16[3,256,1024]{2,1,0:T(8,128)(2,1)S(1)} %get-tuple-element.51.text_parts, f32[256,768]{1,0:T(8,128)S(1)} %collective-permute-done.3.first, f32[256,1024]{1,0:T(8,128)} %get-tuple-element.53.column_store), custom_call_target="tpu_custom_call" | custom-call | flops 805306368 | bytes 4194304 | tf_op jit(solution)/shard_map/pallas_call | solution.py:273
  31.0 0.3 collective-permute-done.4.second
  31.3 3.9 %shard_map.53 = (f32[256,1024]{1,0:T(8,128)}, f32[256,1024]{1,0:T(8,128)}) custom-call(bf16[3,256,1024]{2,1,0:T(8,128)(2,1)S(1)} %get-tuple-element.51.text_parts, bf16[3,256,768]{2,1,0:T(8,128)(2,1)S(1)} %get-tuple-element.54.first_parts, f32[256,256]{1,0:T(8,128)S(1)} %collective-permute-done.4.second, f32[256,256]{1,0:T(8,128)S(1)} %get-tuple-element.56.product, ...), custom_call_target="tpu_custom_call" | custom-call | flops 2415919104 | bytes 4194304 | tf_op jit(solution)/shard_map/pallas_call | solution.py:273
  35.3 0.0 all-to-all-done.messages
  35.3 0.5 %shard_map.54 = f32[1,1]{1,0:T(1,128)} custom-call(f32[32,1,128]{2,1,0:T(1,128)S(1)} %all-to-all-done.messages), custom_call_target="tpu_custom_call" | custom-call | bytes 4194304 | tf_op jit(solution)/shard_map/pallas_call | solution.py:273
Async XLA Ops:
  0.6 18.2 %collective-permute-start = (f32[256,1024]{1,0:T(8,128)}, f32[256,1024]{1,0:T(8,128)S(1)}, u32[]{:S(2)}, u32[]{:S(2)}) collective-permute-start(f32[256,1024]{1,0:T(8,128)} %bitcast.5), channel_id=1, source_target_pairs={{0,2},{2,4},{4,6},{6,8},{8,10},{10,12},{12,14},{14,16},{16,18},{18... | collective-permute-start | bytes 3145736 | tf_op jit(solution)/shard_map/ppermute | solution.py:18
  7.2 11.7 %collective-permute-start.1 = (f32[2,256]{1,0:T(2,128)S(1)}, f32[2,256]{1,0:T(2,128)S(1)}, u32[]{:S(2)}, u32[]{:S(2)}) collective-permute-start(f32[2,256]{1,0:T(2,128)S(1)} %get-tuple-element.37.self_columns), channel_id=1, source_target_pairs={{0,2},{2,4},{4,6},{6,8},{8,10},{10,12},{12,14},{14,16},{16,18},{18... | collective-permute-start | bytes 6152 | tf_op jit(solution)/shard_map/ppermute | solution.py:18
  9.9 3.7 %collective-permute-start.2 = (f32[1,256]{1,0:T(1,128)S(1)}, f32[1,256]{1,0:T(1,128)S(1)}, u32[]{:S(2)}, u32[]{:S(2)}) collective-permute-start(f32[1,256]{1,0:T(1,128)S(1)} %get-tuple-element.38.self_rows), channel_id=1, source_target_pairs={{0,30},{2,0},{4,2},{6,4},{8,6},{10,8},{12,10},{14,12},{16,14},{18,... | collective-permute-start | bytes 3080 | tf_op jit(solution)/shard_map/ppermute | solution.py:18
  18.9 10.9 %collective-permute-start.3 = (f32[256,768]{1,0:T(8,128)S(1)}, f32[256,768]{1,0:T(8,128)S(1)}, u32[]{:S(2)}, u32[]{:S(2)}) collective-permute-start(f32[256,768]{1,0:T(8,128)S(1)} %get-tuple-element.52), channel_id=1, source_target_pairs={{0,30},{2,0},{4,2},{6,4},{8,6},{10,8},{12,10},{14,12},{16,14},{18,... | collective-permute-start | bytes 2359304 | tf_op jit(solution)/shard_map/ppermute | solution.py:18
  20.9 10.4 %collective-permute-start.4 = (f32[256,256]{1,0:T(8,128)S(1)}, f32[256,256]{1,0:T(8,128)S(1)}, u32[]{:S(2)}, u32[]{:S(2)}) collective-permute-start(f32[256,256]{1,0:T(8,128)S(1)} %get-tuple-element.55), channel_id=1, source_target_pairs={{0,30},{2,0},{4,2},{6,4},{8,6},{10,8},{12,10},{14,12},{16,14},{18,... | collective-permute-start | bytes 786440 | tf_op jit(solution)/shard_map/ppermute | solution.py:18
  23.4 11.9 %all-to-all-start = ((f32[32,1,128]{2,1,0:T(1,128)}), f32[32,1,128]{2,1,0:T(1,128)S(1)}, u32[]{:S(2)}, u32[]{:S(2)}) async-start(f32[32,1,128]{2,1,0:T(1,128)} %get-tuple-element.43), calls=%async_computation | async-start | bytes 32768 | tf_op jit(solution)/shard_map/all_to_all | solution.py:317
